TPU v7x, 32 devices: a whole 2x2x4 slice. The times are simulated.
32 devices in a mesh: leaf: 4 (over y, x), row: 4 (over z), col: 2 (over core).
Axes of the slice: x: 2, y: 2, z: 4, core: 2. Of those that a mesh axis runs over, the one named last changes fastest.
Arguments:
- contribution: float32 [4, 10, 4, 128, 40, 2, 128], P('leaf', None, 'row', None, None, 'col'), may hold values from -6 to 6
- panel_left: float32 [4, 10, 4, 128, 2048], P('leaf', None, 'row', None, 'col'), may hold values from -0.1875 to 0.1875
- panel_right: float32 [4, 1024, 40, 2, 128], P('leaf', 'row', None, 'col'), may hold values from -6 to 6
- block_masks: int32 [4, 2, 40, 40], replicated, may hold values 0 or 1
- index_maps: int32 [4, 2, 40], replicated, may hold values from 0 to 63, as said below
- pivot_diag: float32 [512], replicated, may hold values from 80 to 160
Outputs:
- front: float32 [4, 16, 4, 128, 32, 2, 128], P('leaf', None, 'row', None, None, 'col')
Inputs may be any that keep to these rules, and one draw needn't show every extreme that they name: For each child, index_maps[l, s] is one-to-one, and index_maps[l, s, a] is congruent to a modulo 4.
All inputs are finite; a program needn't handle non-finite values.
Results may differ from a plain program's by a relative error of at most 0.0001.
Values sent between devices are 32-bit elements; how exact they have to be, the bound alone decides.
A program may use at most 256 MiB of HBM per device.

v0:
```python
import jax
import jax.numpy as jnp
from jax import lax
from jax.sharding import PartitionSpec as P

BS = 128
CB = 40
PB = 64
PANB = 4
CPAN = 1024
NS_STEPS = 2


def partner(block, axis, stride):
    count = lax.axis_size(axis)
    route = []
    for low in range(count):
        high = low | 1 << stride
        if high != low and high < count:
            route += [(low, high), (high, low)]
    return lax.ppermute(block, axis, route)


def from_root(x, axis, root):
    mine = lax.axis_index(axis) == root
    return lax.psum(jnp.where(mine, x, jnp.zeros_like(x)), axis)


def matmul(first, second):
    return jnp.dot(
        first, second, precision=lax.Precision.HIGHEST, preferred_element_type=jnp.float32
    )


def on_device(contribution, panel_left, panel_right, block_masks, index_maps, pivot_diag):
    row_count = lax.axis_size("row")
    col_count = lax.axis_size("col")
    half_cols = col_count // 2
    leaf_index = lax.axis_index("leaf")
    row_index = lax.axis_index("row")
    col_index = lax.axis_index("col")
    child_side = col_index // half_cols
    group_index = col_index % half_cols
    child_rows = contribution.shape[1]
    child_cols = contribution.shape[4]
    parent_rows = PB // row_count
    parent_cols = PB // col_count
    width = PANB * BS
    cmat = contribution.reshape(child_rows * BS, child_cols * BS)
    gathered_right = lax.all_gather(panel_right, "row", axis=1, tiled=True)
    right = gathered_right.reshape(CPAN, child_cols * BS)
    gathered_left = lax.all_gather(panel_left, "col", axis=4, tiled=True)
    paired = gathered_left.reshape(child_rows * BS, CPAN, 2)
    first_child = paired[:, :, 0]
    second_child = paired[:, :, 1]
    left = jnp.where(child_side == 0, first_child, second_child)
    product = matmul(left, right)
    own_mask = block_masks[leaf_index, child_side]
    own_mask = own_mask.reshape(child_rows, row_count, CB)[:, row_index]
    own_mask = own_mask.reshape(child_rows, child_cols, half_cols)[:, :, group_index].astype(
        jnp.float32
    )
    schur = (cmat - product).reshape(child_rows, BS, child_cols, BS) * own_mask[:, None, :, None]
    own_map = index_maps[leaf_index, child_side]
    target = own_map.reshape(child_cols, half_cols)[:, group_index]
    stays = (target % col_count // half_cols == child_side).astype(jnp.float32)
    kept_here = schur * stays[None, None, :, None]
    leaving = schur * (1.0 - stays)[None, None, :, None]
    top_bit = col_count.bit_length() - 2
    arrived = partner(leaving, "col", top_bit)
    outgoing = jnp.where(child_side == 0, arrived, kept_here)
    staying = jnp.where(child_side == 0, kept_here, arrived)
    incoming = partner(outgoing, "leaf", 0)

    def assemble(piece, mapping):
        row_map = mapping.reshape(child_rows, row_count)[:, row_index] // row_count
        row_select = (row_map[None, :] == jnp.arange(parent_rows)[:, None]).astype(jnp.float32)
        col_map = mapping.reshape(child_cols, half_cols)[:, group_index]
        wanted = jnp.arange(parent_cols) * col_count + col_index
        col_select = (col_map[None, :] == wanted[:, None]).astype(jnp.float32)
        placed = jnp.einsum("pk,kxly->pxly", row_select, piece, precision=lax.Precision.HIGHEST)
        return jnp.einsum("pxly,ql->pxqy", placed, col_select, precision=lax.Precision.HIGHEST)

    first_map = index_maps[leaf_index, 0]
    second_map = index_maps[jnp.bitwise_xor(leaf_index, 1), 1]
    assembled = assemble(staying, first_map) + assemble(incoming, second_map)
    row_blocks = jnp.arange(parent_rows) * row_count + row_index
    col_blocks = jnp.arange(parent_cols) * col_count + col_index
    on_pivot = ((row_blocks[:, None] == col_blocks[None, :]) & (row_blocks[:, None] < PANB)).astype(
        jnp.float32
    )
    diag_rows = pivot_diag.reshape(PANB, BS)[jnp.clip(row_blocks, 0, PANB - 1)]
    identity = jnp.eye(BS, dtype=jnp.float32)
    assembled = assembled + on_pivot[:, None, :, None] * (
        diag_rows[:, :, None, None] * identity[None, :, None, :]
    )
    column_parts = []
    for block in range(PANB):
        owned = assembled[:, :, block // col_count, :]
        column_parts.append(from_root(owned, "col", block % col_count))
    western_raw = jnp.stack(column_parts, axis=2).reshape(parent_rows, BS, width)
    pieces_row = PANB // row_count
    north_raw = lax.all_gather(assembled[:pieces_row], "row", axis=0, tiled=True)
    north_raw = north_raw.reshape(row_count, pieces_row, BS, parent_cols * BS)
    north_raw = jnp.transpose(north_raw, (1, 0, 2, 3)).reshape(width, parent_cols * BS)
    pivot = lax.all_gather(western_raw[:pieces_row], "row", axis=0, tiled=True)
    pivot = jnp.transpose(pivot.reshape(row_count, pieces_row, BS, width), (1, 0, 2, 3)).reshape(
        width, width
    )
    inverse = jnp.diag(1.0 / pivot_diag)
    for sweep in range(NS_STEPS):
        inverse = 2.0 * inverse - matmul(matmul(inverse, pivot), inverse)
    western = (western_raw * (row_blocks >= PANB).astype(jnp.float32)[:, None, None]).reshape(
        parent_rows * BS, width
    )
    col_keep = jnp.repeat((col_blocks >= PANB).astype(jnp.float32), BS)
    northern = north_raw * col_keep[None, :]
    update = matmul(matmul(western, inverse), northern)
    result = assembled.reshape(parent_rows * BS, parent_cols * BS) - update
    keep_mask = ((row_blocks >= PANB)[:, None] & (col_blocks >= PANB)[None, :]).astype(jnp.float32)
    result = result.reshape(parent_rows, BS, parent_cols, BS) * keep_mask[:, None, :, None]
    return result.reshape(1, parent_rows, 1, BS, parent_cols, 1, BS)


def solution(mesh):
    placed = (
        P("leaf", None, "row", None, None, "col", None),
        P("leaf", None, "row", None, "col"),
        P("leaf", "row", None, "col", None),
        P(),
        P(),
        P(),
    )
    return jax.shard_map(
        on_device,
        mesh=mesh,
        in_specs=placed,
        out_specs=P("leaf", None, "row", None, None, "col", None),
        check_vma=False,
    )
```

profile of v0, /device:TPU:0, one launch (start us, length us, event | category | flops | bytes accessed | tf_op | source)
XLA Modules:
  0.0 1666.9 jit_solution(12787175434399094191)
XLA Ops:
  6.5 0.0 copy-start
  6.5 0.0 all-gather.5.cloned.1.call-start
  6.5 0.7 all-gather.5.cloned.1.call-update
  7.3 0.0 all-gather.7.cloned.1.call-start
  7.3 0.7 all-gather.7.cloned.1.call-update
  8.0 0.0 all-reduce.3.cloned.1.call-start
  8.1 0.0 copy-done
  8.1 0.7 broadcast_subtract_fusion
  8.8 25.7 %all-gather.5.cloned.1.call-done = f32[1,10,1,128,2048]{4,3,2,1,0:T(8,128)} async-done(((f32[1,10,1,128,1024]{4,3,2,1,0:T(8,128)}), f32[1,10,1,128,2048]{4,3,2,1,0:T(8,128)}) %all-gather.5.cloned.1.call-update) | async-done | bytes 10485776 | tf_op jit(solution)/shard_map/all_gather | solution.py:52
  34.5 17.9 %copy.19 = f32[1,10,1,128,2048]{3,1,4,2,0:T(8,128)} copy(f32[1,10,1,128,2048]{4,3,2,1,0:T(8,128)} %all-gather.5.cloned.1.call-done) | data formatting | bytes 20971520 | tf_op jit(solution)/shard_map/all_gather | solution.py:52
  52.4 17.1 %reshape.289 = f32[1280,1024,2]{0,2,1:T(2,128)} reshape(f32[1,10,1,128,2048]{3,1,4,2,0:T(8,128)} %copy.19) | data formatting | bytes 20971520 | tf_op jit(solution)/shard_map/reshape | solution.py:53
  69.5 11.7 broadcast_select_fusion
  81.2 11.6 copy.20
  92.9 301.3 %all-gather.7.cloned.1.call-done = f32[1,1024,40,1,128]{4,2,3,0,1:T(8,128)} async-done(((f32[1,256,40,1,128]{4,2,3,0,1:T(8,128)}), f32[1,1024,40,1,128]{4,2,3,0,1:T(8,128)}) %all-gather.7.cloned.1.call-update) | async-done | bytes 20971536 | tf_op jit(solution)/shard_map/all_gather | solution.py:50
  394.1 109.0 %fusion.9 = f32[160,8,40,128]{3,1,2,0:T(8,128)} fusion(f32[160,8,40,128]{3,2,1,0:T(8,128)} %bitcast.129, f32[128,8,40,128]{3,2,1,0:T(8,128)} %bitcast.130, f32[1280,1024,1]{1,0,2:T(8,128)} %copy.20), kind=kOutput, calls=%fused_computation.14 | convolution fusion | flops 80537190400 | bytes 78643200 | tf_op jit(solution)/shard_map/dot_general | solution.py:30
  503.2 13.8 copy.34
  517.0 0.0 copy-start.2
  517.0 11.0 fusion.10
  528.0 5.5 copy-done.2
  533.5 0.0 collective-permute-start
  533.5 39.0 %collective-permute-done = f32[10,128,40,128]{3,2,1,0:T(8,128)} collective-permute-done((f32[10,128,40,128]{3,2,1,0:T(8,128)}, f32[10,128,40,128]{3,2,1,0:T(8,128)}, u32[]{:S(2)}, u32[]{:S(2)}) %collective-permute-start) | collective-permute-done | bytes 26214432 | tf_op jit(solution)/shard_map/ppermute | solution.py:21
  572.5 0.0 copy-start.4
  572.5 34.1 %fusion.13 = (f32[10,128,40,128]{3,2,1,0:T(8,128)}, f32[10,128,40,128]{3,2,1,0:T(8,128)}) fusion(f32[10,128,40,128]{3,2,1,0:T(8,128)} %collective-permute-done, f32[40]{0:T(128)S(1)} %get-tuple-element.12, f32[10,40]{1,0:T(8,128)S(1)} %bitcast.127, pred[]{:T(512)S(6)} %eq.117, f32[10,128,40,128]{3,2,1,0:T(8,128)} %bitcast.117), kind=kLoop, calls=%fused_computation.18 | loop fusion | flops 26214400 | bytes 104859360 | tf_op jit(solution)/shard_map/jit(_where)/select_n | solution.py:72
  606.6 1.5 collective-permute-start.1
  608.1 0.7 fusion.53
  608.8 0.1 reshape_squeeze.15
  608.9 0.1 reshape_squeeze.6
  609.0 0.0 copy-done.4
  609.0 0.6 gather_fusion
  609.5 0.2 dynamic-slice_reduce_fusion
  609.7 0.2 dynamic-slice_reduce_fusion.1
  610.0 0.1 and_convert_fusion.1
  610.1 0.3 broadcast_multiply_fusion.1
  610.4 44.9 %fusion.6 = f32[16,128,40,128]{3,0,2,1:T(8,128)} fusion(f32[10,128,40,128]{3,2,1,0:T(8,128)} %get-tuple-element.13, s32[10]{0:T(128)S(1)} %get-tuple-element.22), kind=kOutput, calls=%fused_computation.7 | convolution fusion | flops 1258291328 | bytes 68157480 | tf_op jit(solution)/shard_map/pk,kxly->pxly/dot_general | solution.py:81
  655.3 516.1 %collective-permute-done.1 = f32[10,128,40,128]{3,2,1,0:T(8,128)} collective-permute-done((f32[10,128,40,128]{3,2,1,0:T(8,128)}, f32[10,128,40,128]{3,2,1,0:T(8,128)}, u32[]{:S(2)}, u32[]{:S(2)}) %collective-permute-start.1) | collective-permute-done | bytes 26214432 | tf_op jit(solution)/shard_map/ppermute | solution.py:21
  1171.4 45.1 %fusion.2 = f32[16,128,40,128]{3,0,2,1:T(8,128)} fusion(f32[10,128,40,128]{3,2,1,0:T(8,128)} %collective-permute-done.1, s32[10]{0:T(128)S(1)} %get-tuple-element.21), kind=kOutput, calls=%fused_computation.3 | convolution fusion | flops 1258291328 | bytes 68157480 | tf_op jit(solution)/shard_map/pk,kxly->pxly/dot_general | solution.py:81
  1216.5 38.3 %fusion = f32[32,16,128,128]{3,0,2,1:T(8,128)} fusion(f32[16,128,40,128]{3,0,2,1:T(8,128)} %fusion.2, s32[40]{0:T(128)S(1)} %get-tuple-element.20, s32[32]{0:T(128)S(1)} %multiply_add_fusion.1), kind=kOutput, calls=%fused_computation.1 | convolution fusion | flops 4026533120 | bytes 75497760 | tf_op jit(solution)/shard_map/pxly,ql->pxqy/dot_general | solution.py:82
  1254.8 51.8 %bitcast_add_fusion = f32[16,128,32,128]{3,2,1,0:T(8,128)} fusion(f32[32,16,128,128]{3,0,2,1:T(8,128)} %fusion, f32[16,128,128]{2,1,0:T(8,128)S(1)} %broadcast_multiply_fusion.1, f32[16,32]{1,0:T(8,128)S(1)} %and_convert_fusion.1, f32[16,128,40,128]{3,0,2,1:T(8,128)} %fusion.6, s32[40]{0:T(128)S(1)} %get-tuple-element.19, s32[32]{0:T(128)S(1)} %multiply_add_fusion.1), kind=kOutput, calls=%fused_computation.11 | convolution fusion | flops 4051698944 | bytes 110102816 | tf_op jit(solution)/shard_map/pxly,ql->pxqy/dot_general | solution.py:82
  1306.7 9.3 broadcast_select_fusion.4
  1316.0 0.0 all-reduce.3.cloned.1.call-update
  1316.0 0.0 all-gather.9.cloned.1.call-start
  1316.1 27.4 %all-reduce.3.cloned.1.call-done = (f32[16,128,1,128]{3,2,1,0:T(1,128)}, f32[16,128,1,128]{3,2,1,0:T(1,128)}, f32[16,128,1,128]{3,2,1,0:T(1,128)}, f32[16,128,1,128]{3,2,1,0:T(1,128)}) async-done(((f32[16,128,1,128]{3,2,1,0:T(1,128)}, f32[16,128,1,128]{3,2,1,0:T(1,128)}, f32[16,128,1,128]{3,2,1,0:T(1,128)}, f32[16,128,1,128]{3,2,1,0:T(1,128)}), (f32[16,128,1,128]{3,2,1,0:T(1,128)}, ...) | async-done | bytes 4194320 | tf_op jit(solution)/shard_map/psum | solution.py:26
  1343.5 6.1 pad_maximum_fusion
  1349.6 0.0 copy-start.3
  1349.6 1.9 copy-done.3
  1351.6 0.8 slice.28
  1352.4 0.0 all-gather.9.cloned.1.call-update
  1352.4 0.0 all-gather.11.cloned.1.call-start
  1352.5 3.1 slice.37
  1355.6 0.0 all-gather.11.cloned.1.call-update
  1355.7 0.1 broadcast_bitcast_fusion.1
  1355.7 0.1 and_convert_fusion
  1355.8 0.1 broadcast_bitcast_fusion
  1355.9 25.8 %all-gather.9.cloned.1.call-done = f32[4,128,512]{2,1,0:T(8,128)} async-done(((f32[1,128,512]{2,1,0:T(8,128)}), f32[4,128,512]{2,1,0:T(8,128)}) %all-gather.9.cloned.1.call-update) | async-done | bytes 1048592 | tf_op jit(solution)/shard_map/all_gather | solution.py:106
  1381.7 3.1 fusion.26
  1384.8 1.9 fusion.28
  1386.6 3.1 fusion.61
  1389.7 1.9 convolution_subtract_fusion
  1391.6 10.5 fusion.20
  1402.1 130.2 %all-gather.11.cloned.1.call-done = f32[4,128,32,128]{3,2,1,0:T(8,128)} async-done(((f32[1,128,32,128]{3,2,1,0:T(8,128)}), f32[4,128,32,128]{3,2,1,0:T(8,128)}) %all-gather.11.cloned.1.call-update) | async-done | bytes 8388624 | tf_op jit(solution)/shard_map/all_gather | solution.py:103
  1532.4 68.2 %fusion.8 = f32[256,8,32,128]{3,1,2,0:T(8,128)} fusion(f32[256,8,32,128]{3,2,1,0:T(8,128)} %bitcast.118, f32[2048,512]{1,0:T(8,128)} %fusion.20, f32[64,8,32,128]{3,2,1,0:T(8,128)} %bitcast.121, f32[4096]{0:T(1024)S(1)} %broadcast_bitcast_fusion), kind=kOutput, calls=%fused_computation.10 | convolution fusion | flops 51550093312 | bytes 79708160 | tf_op jit(solution)/shard_map/dot_general | solution.py:30
  1600.6 27.6 %copy.38 = f32[256,8,32,128]{3,2,1,0:T(8,128)} copy(f32[256,8,32,128]{3,1,2,0:T(8,128)} %fusion.8) | data formatting | bytes 67108864
  1628.2 31.9 %broadcast_multiply_fusion = f32[1,16,1,128,32,1,128]{6,5,4,3,2,1,0:T(1,128)} fusion(f32[1,16,1,128,32,1,128]{6,5,4,3,2,1,0:T(1,128)} %bitcast.119, f32[16,32]{1,0:T(8,128)S(1)} %and_convert_fusion), kind=kLoop, calls=%fused_computation.21 | loop fusion | flops 8388608 | bytes 67110912 | tf_op jit(solution)/shard_map/mul | solution.py:121
  1660.1 0.0 copy-done.1
  (17 shorter events, 0.1 us)
Async XLA Ops:
  6.5 1.5 copy-start
  6.5 28.0 %all-gather.5.cloned.1.call-start = ((), (), s32[]{:S(2)}) async-start(), calls=%async_computation | async-start | bytes 15728640 | tf_op jit(solution)/shard_map/all_gather | solution.py:52
  7.3 386.9 %all-gather.7.cloned.1.call-start = ((), (), s32[]{:S(2)}) async-start(), calls=%async_computation.1 | async-start | bytes 26214400 | tf_op jit(solution)/shard_map/all_gather | solution.py:50
  8.0 1335.5 %all-reduce.3.cloned.1.call-start = ((), (), s32[]{:S(2)}) async-start(), calls=%async_computation.4 | async-start | bytes 8388608 | tf_op jit(solution)/shard_map/psum | solution.py:26
  517.0 16.5 copy-start.2
  533.5 39.0 %collective-permute-start = (f32[10,128,40,128]{3,2,1,0:T(8,128)}, f32[10,128,40,128]{3,2,1,0:T(8,128)}, u32[]{:S(2)}, u32[]{:S(2)}) collective-permute-start(f32[10,128,40,128]{3,2,1,0:T(8,128)} %fusion.10), channel_id=1, source_target_pairs={{0,1},{1,0},{2,3},{3,2},{4,5},{5,4},{6,7},{7,6},{8,9},{9,8},{10,11... | collective-permute-start | bytes 78643208 | tf_op jit(solution)/shard_map/ppermute | solution.py:21
  572.5 36.5 %copy-start.4 = (f32[512]{0:T(512)S(1)}, f32[512]{0:T(512)}, u32[]{:S(2)}) copy-start(f32[512]{0:T(512)} %param.11) | copy-start | bytes 6148
  606.6 564.8 %collective-permute-start.1 = (f32[10,128,40,128]{3,2,1,0:T(8,128)}, f32[10,128,40,128]{3,2,1,0:T(8,128)}, u32[]{:S(2)}, u32[]{:S(2)}) collective-permute-start(f32[10,128,40,128]{3,2,1,0:T(8,128)} %get-tuple-element.14), channel_id=1, source_target_pairs={{0,8},{8,0},{16,24},{24,16},{1,9},{9,1},{17,25},{25,17},{2,10},{10... | collective-permute-start | bytes 78643208 | tf_op jit(solution)/shard_map/ppermute | solution.py:21
  1316.0 65.7 %all-gather.9.cloned.1.call-start = ((), (), s32[]{:S(2)}) async-start(), calls=%async_computation.2 | async-start | bytes 1310720 | tf_op jit(solution)/shard_map/all_gather | solution.py:106
  1349.6 1.9 copy-start.3
  1352.4 179.9 %all-gather.11.cloned.1.call-start = ((), (), s32[]{:S(2)}) async-start(), calls=%async_computation.3 | async-start | bytes 10485760 | tf_op jit(solution)/shard_map/all_gather | solution.py:103
  1628.2 32.0 %copy-start.1 = (s32[4,2,40,40]{3,2,1,0:T(8,128)S(1)}, s32[4,2,40,40]{3,2,1,0:T(8,128)}, u32[]{:S(2)}) copy-start(s32[4,2,40,40]{3,2,1,0:T(8,128)} %param.9) | copy-start | bytes 153604
Sparse Core Ops, SparseCore 0:
  8.9 25.5 all-gather.4
  36.1 357.9 all-gather.6
  1316.2 27.2 all-reduce.2
  1352.6 29.0 all-gather.8
  1383.2 149.1 all-gather.10
where the time goes:
time: 1680 us; the launch traced here: 1670 us
  waiting for transfers between devices  1070 us (64%)
  matrix products  378 us (22%)
  other arithmetic  106 us (6%)
  local copies, waits for them, and re-layouts  101 us (6%)
    ppermute x2, waiting for transfers between devices, partner(): return lax.ppermute(block, axis, route)  555 us
    all_gather x1, waiting for transfers between devices, on_device(): gathered_right = lax.all_gather(panel_right, 'row', axis=1, tiled=True)  301 us
    dot_general x7, matrix products, matmul(): jnp.dot(first, second, precision=lax.Precision.HIGHEST, preferred_element...  198 us
    all_gather x1, waiting for transfers between devices, on_device(): lax.all_gather(assembled[:pieces_row], 'row', axis=0, tiled=True)  130 us
    dot_general x2, matrix products, assemble(): jnp.einsum('pxly,ql->pxqy', placed, col_select, precision=lax.Precision.H...  90.1 us
    dot_general x2, matrix products, assemble(): jnp.einsum('pk,kxly->pxly', row_select, piece, precision=lax.Precision.HI...  90.1 us
    unnamed x13, local copies, waits for them, and re-layouts  48.8 us
    select_n x1, other arithmetic, on_device(): staying = jnp.where(child_side == 0, kept_here, arrived)  34.1 us
  transfers between devices with their start and end apart: 7, of which 7 were waited for; matrix products, arithmetic and copies ran while one was open for 8% of the time, Pallas kernels for 0%

commit v1 on v0

--- a/solution.py
+++ b/solution.py
@@ -1,6 +1,10 @@
+import functools
+
 import jax
 import jax.numpy as jnp
 from jax import lax
+from jax.experimental import pallas as pl
+from jax.experimental.pallas import tpu as pltpu
 from jax.sharding import PartitionSpec as P
 
 BS = 128
@@ -32,7 +36,7 @@
     )
 
 
-def on_device(contribution, panel_left, panel_right, block_masks, index_maps, pivot_diag):
+def on_device_general(contribution, panel_left, panel_right, block_masks, index_maps, pivot_diag):
     row_count = lax.axis_size("row")
     col_count = lax.axis_size("col")
     half_cols = col_count // 2
@@ -122,6 +126,309 @@
     return result.reshape(1, parent_rows, 1, BS, parent_cols, 1, BS)
 
 
+GROUP = 8
+VMEM_LIMIT = 60 * 1024 * 1024
+
+
+def split(x):
+    high = lax.reduce_precision(x, 8, 7)
+    return high.astype(jnp.bfloat16), (x - high).astype(jnp.bfloat16)
+
+
+def split_in_kernel(x):
+    high = x.astype(jnp.bfloat16)
+    return high, (x - high.astype(jnp.float32)).astype(jnp.bfloat16)
+
+
+def dot3(a_high, a_low, b_high, b_low):
+    dot = functools.partial(jnp.dot, preferred_element_type=jnp.float32)
+    return dot(a_high, b_high) + (dot(a_high, b_low) + dot(a_low, b_high))
+
+
+def schur_kernel(chunk, rows_at_once, side_ref, mask_ref, lh_ref, ll_ref, r_ref, c_ref, own_ref, send_ref):
+    side = side_ref[0]
+    rows, depth = lh_ref.shape
+    r_flat = r_ref.reshape(depth * GROUP, BS)
+    c_flat = c_ref.reshape(rows * GROUP, BS)
+    for pair in range(GROUP // 2):
+        q_own = 2 * pair + side
+        q_send = 2 * pair + 1 - side
+        right = jnp.concatenate(
+            [r_flat[pl.ds(q, depth, stride=GROUP), :] for q in (q_own, q_send)], axis=1
+        )
+        right_high, right_low = split_in_kernel(right)
+
+        def body(step, carry):
+            start = pl.multiple_of(step * rows_at_once, rows_at_once)
+            lines = pl.ds(start, rows_at_once)
+            product = dot3(lh_ref[lines, :], ll_ref[lines, :], right_high, right_low)
+            for place, (q, out_ref) in enumerate(((q_own, own_ref), (q_send, send_ref))):
+                c_part = c_flat[pl.ds(start * GROUP + q, rows_at_once, stride=GROUP), :]
+                value = c_part - product[:, place * BS : (place + 1) * BS]
+                for block in range(rows_at_once // BS):
+                    keep = mask_ref[step * (rows_at_once // BS) + block, chunk * GROUP + q]
+                    out_ref[pair, pl.ds(start + block * BS, BS), :] = value[
+                        block * BS : (block + 1) * BS
+                    ] * keep.astype(jnp.float32)
+            return carry
+
+        lax.fori_loop(0, rows // rows_at_once, body, 0)
+
+
+def schur_chunk(chunk, side, mask, left_high, left_low, right, cmat):
+    rows, depth = left_high.shape
+    half = jax.ShapeDtypeStruct((GROUP // 2, rows, BS), jnp.float32)
+    whole = lambda shape: pl.BlockSpec(shape, lambda i, *_: (0,) * len(shape))
+    rows_at_once = 2 * BS if rows % (2 * BS) == 0 else BS
+    return pl.pallas_call(
+        functools.partial(schur_kernel, chunk, rows_at_once),
+        out_shape=(half, half),
+        grid_spec=pltpu.PrefetchScalarGridSpec(
+            num_scalar_prefetch=2,
+            grid=(1,),
+            in_specs=[
+                whole((rows, depth)),
+                whole((rows, depth)),
+                whole((depth, GROUP, BS)),
+                pl.BlockSpec((rows, GROUP, BS), lambda i, *_: (0, chunk, 0)),
+            ],
+            out_specs=[whole(half.shape), whole(half.shape)],
+        ),
+        compiler_params=pltpu.CompilerParams(vmem_limit_bytes=VMEM_LIMIT),
+        cost_estimate=pl.CostEstimate(
+            flops=6 * rows * depth * GROUP * BS,
+            bytes_accessed=4 * (rows * depth + depth * GROUP * BS + 2 * rows * GROUP * BS),
+            transcendentals=0,
+        ),
+        name="schur_chunk",
+    )(side, mask, left_high, left_low, right, cmat)
+
+
+def update_kernel(first_keep, panel_cols, row_step, first_col, first_colok, second_col, second_colok, first_row, first_rowok, second_row, second_rowok, *refs):
+    first = refs[:GROUP]
+    second = refs[GROUP : 2 * GROUP]
+    wh_ref, wl_ref = refs[2 * GROUP : 2 * GROUP + 2]
+    v_refs = refs[2 * GROUP + 2 : 2 * GROUP + 2 + GROUP // 2]
+    out_ref = refs[-1]
+    rows, width = wh_ref.shape
+    out_flat = out_ref.reshape(rows * GROUP, BS)
+    group = pl.program_id(0)
+    blocks = row_step // BS
+    for pair in range(GROUP // 2):
+        v_ref = v_refs[pair]
+        v = jnp.concatenate([v_ref[:, i].reshape(width, BS) for i in range(2)], axis=1)
+        v_high, v_low = split_in_kernel(v)
+
+        def body(step, carry):
+            lines = pl.ds(pl.multiple_of(step * row_step, row_step), row_step)
+            product = dot3(wh_ref[lines, :], wl_ref[lines, :], v_high, v_low)
+            for block in range(blocks):
+                k = step * blocks + block
+                for i in range(2):
+                    place = 2 * pair + i
+                    q = group * GROUP + place
+                    keep = jnp.where((k >= first_keep) & (q >= panel_cols), 1.0, 0.0).astype(
+                        jnp.float32
+                    )
+                    total = -product[block * BS : (block + 1) * BS, i * BS : (i + 1) * BS]
+                    for slabs, col_ok, row_at, row_ok in (
+                        (first, first_colok, first_row, first_rowok),
+                        (second, second_colok, second_row, second_rowok),
+                    ):
+                        use = (col_ok[q] * row_ok[k]).astype(jnp.float32)
+                        from_row = pl.multiple_of(row_at[k] * BS, BS)
+                        total = total + slabs[place][0, pl.ds(from_row, BS), :] * use
+                    out_flat[pl.ds(k * (BS * GROUP) + place, BS, stride=GROUP), :] = total * keep
+            return carry
+
+        lax.fori_loop(0, rows // row_step, body, 0)
+
+
+def update(first_keep, panel_cols, scalars, first, second, w_high, w_low, northern, parent_cols):
+    rows, width = w_high.shape
+    child_rows = first.shape[1]
+    pieces = northern.shape[0]
+    row_step = 4 * BS if rows % (4 * BS) == 0 else BS
+
+    def slab(which, place):
+        def at(g, *prefetched):
+            return prefetched[which][g * GROUP + place], 0, 0
+
+        return pl.BlockSpec((1, child_rows, BS), at)
+
+    def north(pair):
+        def at(g, *_):
+            return 0, jnp.maximum(g * (GROUP // 2) + pair - panel_cols // 2, 0), 0, 0
+
+        return pl.BlockSpec((pieces, 2, BS, BS), at)
+
+    whole = pl.BlockSpec((rows, width), lambda g, *_: (0, 0), pipeline_mode=pl.Buffered(1))
+    return pl.pallas_call(
+        functools.partial(update_kernel, first_keep, panel_cols, row_step),
+        out_shape=jax.ShapeDtypeStruct((rows, parent_cols, BS), jnp.float32),
+        grid_spec=pltpu.PrefetchScalarGridSpec(
+            num_scalar_prefetch=8,
+            grid=(parent_cols // GROUP,),
+            in_specs=[slab(0, i) for i in range(GROUP)]
+            + [slab(2, i) for i in range(GROUP)]
+            + [whole, whole]
+            + [north(i) for i in range(GROUP // 2)],
+            out_specs=pl.BlockSpec((rows, GROUP, BS), lambda g, *_: (0, g, 0)),
+        ),
+        compiler_params=pltpu.CompilerParams(vmem_limit_bytes=VMEM_LIMIT),
+        cost_estimate=pl.CostEstimate(
+            flops=6 * rows * width * parent_cols * BS,
+            bytes_accessed=4 * (2 * child_rows + rows + width) * parent_cols * BS,
+            transcendentals=0,
+        ),
+        name="front_update",
+    )(*scalars, *([first] * GROUP), *([second] * GROUP), w_high, w_low, *([northern] * (GROUP // 2)))
+
+
+def inverse_map(targets, count):
+    hits = targets[None, :] == jnp.arange(count, dtype=jnp.int32)[:, None]
+    return jnp.argmax(hits, axis=1).astype(jnp.int32), jnp.any(hits, axis=1).astype(jnp.int32)
+
+
+def on_device_paired(contribution, panel_left, panel_right, block_masks, index_maps, pivot_diag):
+    row_count = lax.axis_size("row")
+    col_count = lax.axis_size("col")
+    leaf_index = lax.axis_index("leaf")
+    row_index = lax.axis_index("row")
+    side = lax.axis_index("col")
+    child_rows = contribution.shape[1]
+    child_cols = contribution.shape[4]
+    blocks = child_rows * row_count
+    rows = child_rows * BS
+    parent_rows = PB // row_count
+    parent_cols = PB // col_count
+    width = PANB * BS
+    panel_rows = PANB // row_count
+    panel_cols = PANB // col_count
+    exact = lax.Precision.HIGHEST
+
+    cmat = contribution.reshape(rows, child_cols, BS)
+    right_local = panel_right.reshape(panel_right.shape[1], child_cols, BS)
+    depth = right_local.shape[0] * row_count
+    chunks = child_cols // GROUP
+
+    gathered = []
+    for chunk in range(chunks):
+        piece = right_local[:, chunk * GROUP : (chunk + 1) * GROUP]
+        if gathered:
+            piece, gathered[-1] = lax.optimization_barrier((piece, gathered[-1]))
+        gathered.append(lax.all_gather(piece, "row", axis=0, tiled=True))
+
+    local_left = panel_left.reshape(rows, panel_left.shape[4])
+    local_depth = local_left.shape[1] // 2
+    line = jnp.arange(2 * local_depth)[:, None]
+    pick = 2 * jnp.arange(local_depth)[None, :]
+    kept = matmul(local_left, (line == pick + side).astype(jnp.float32))
+    given = matmul(local_left, (line == pick + 1 - side).astype(jnp.float32))
+    taken = partner(given, "col", 0)
+    left = jnp.where(
+        side == 0,
+        jnp.concatenate([kept, taken], axis=1),
+        jnp.concatenate([taken, kept], axis=1),
+    )
+    left_high, left_low = split(left)
+
+    mask = block_masks[leaf_index, side].reshape(child_rows, row_count, blocks)[:, row_index]
+    side_arg = side.astype(jnp.int32).reshape(1)
+    first = jnp.zeros((child_cols // 2, rows, BS), jnp.float32)
+    second = jnp.zeros((child_cols // 2, rows, BS), jnp.float32)
+    for chunk in range(chunks):
+        own, sent = schur_chunk(chunk, side_arg, mask, left_high, left_low, gathered[chunk], cmat)
+        got = partner(sent, "col", 0)
+        incoming = partner(jnp.where(side == 0, got, own), "leaf", 0)
+        at = chunk * (GROUP // 2)
+        first = lax.dynamic_update_slice(first, jnp.where(side == 0, own, got), (at, 0, 0))
+        second = lax.dynamic_update_slice(second, incoming, (at, 0, 0))
+
+    maps = (index_maps[leaf_index, 0], index_maps[jnp.bitwise_xor(leaf_index, 1), 1])
+    row_targets = [
+        m.reshape(child_rows, row_count)[:, row_index].astype(jnp.int32) // row_count for m in maps
+    ]
+    col_targets = [
+        m.reshape(child_cols // 2, 2)[:, side].astype(jnp.int32) // col_count for m in maps
+    ]
+    cols = [inverse_map(t, parent_cols) for t in col_targets]
+    lines = [inverse_map(t, parent_rows) for t in row_targets]
+    children = (first, second)
+
+    identity = jnp.eye(BS, dtype=jnp.float32)
+    diag = pivot_diag.reshape(PANB, BS)
+    col_blocks = jnp.arange(parent_cols) * col_count + side
+
+    north_local = []
+    for piece in range(panel_rows):
+        strip = jnp.zeros((parent_cols, BS, BS), jnp.float32)
+        for child, (at, ok), target in zip(children, lines, col_targets):
+            taken_rows = lax.dynamic_slice(
+                child, (0, at[piece] * BS, 0), (child.shape[0], BS, BS)
+            ) * ok[piece].astype(jnp.float32)
+            select = (target[None, :] == jnp.arange(parent_cols)[:, None]).astype(jnp.float32)
+            strip = strip + jnp.einsum("qj,jxy->qxy", select, taken_rows, precision=exact)
+        row_block = piece * row_count + row_index
+        on_pivot = (col_blocks == row_block).astype(jnp.float32)
+        strip = strip + on_pivot[:, None, None] * (diag[row_block][:, None] * identity)[None]
+        north_local.append(strip)
+    north_local = jnp.stack(north_local)
+
+    corner = lax.all_gather(north_local[:, :panel_cols], "row", axis=1)
+    trailing, corner = lax.optimization_barrier((north_local[:, panel_cols:], corner))
+    northern = lax.all_gather(trailing, "row", axis=1)
+    northern = northern.reshape(PANB, parent_cols - panel_cols, BS, BS)
+
+    def both_sides(mine):
+        other = partner(mine, "col", 0)
+        return jnp.where(side == 0, jnp.stack([mine, other]), jnp.stack([other, mine]))
+
+    corner = corner.reshape(PANB, panel_cols, BS, BS)
+    pivot = jnp.transpose(both_sides(corner), (1, 3, 2, 0, 4)).reshape(width, width)
+
+    west = jnp.zeros((panel_cols, parent_rows, BS, BS), jnp.float32)
+    for child, (at, ok), target in zip(children, cols, row_targets):
+        slabs = jnp.stack(
+            [
+                lax.dynamic_slice(child, (at[i], 0, 0), (1, rows, BS))[0]
+                * ok[i].astype(jnp.float32)
+                for i in range(panel_cols)
+            ]
+        ).reshape(panel_cols, child_rows, BS, BS)
+        select = (target[None, :] == jnp.arange(parent_rows)[:, None]).astype(jnp.float32)
+        west = west + jnp.einsum("pk,qkxy->qpxy", select, slabs, precision=exact)
+    below = (jnp.arange(parent_rows) >= panel_rows).astype(jnp.float32)
+    west = west * below[None, :, None, None]
+    western = jnp.transpose(both_sides(west), (2, 3, 1, 0, 4)).reshape(parent_rows * BS, width)
+
+    inverse = jnp.diag(1.0 / pivot_diag)
+    for sweep in range(NS_STEPS):
+        inverse = 2.0 * inverse - matmul(matmul(inverse, pivot), inverse)
+    scaled_high, scaled_low = split(matmul(western, inverse))
+
+    scalars = (*cols[0], *cols[1], *lines[0], *lines[1])
+    result = update(
+        panel_rows, panel_cols, scalars, first, second, scaled_high, scaled_low, northern, parent_cols
+    )
+    return result.reshape(1, parent_rows, 1, BS, parent_cols, 1, BS)
+
+
+def on_device(contribution, *others):
+    row_count = lax.axis_size("row")
+    col_count = lax.axis_size("col")
+    paired = (
+        col_count == 2
+        and row_count % 2 == 0
+        and PANB % row_count == 0
+        and (PANB // col_count) % 2 == 0
+        and contribution.shape[4] % GROUP == 0
+        and (PB // col_count) % GROUP == 0
+    )
+    chosen = on_device_paired if paired else on_device_general
+    return chosen(contribution, *others)
+
+
 def solution(mesh):
     placed = (
         P("leaf", None, "row", None, None, "col", None),

time: 1680 us -> 983 us (0.59)
  waiting for transfers between devices: 1070 us -> 657 us
  matrix products: 378 us -> 40.4 us
  Pallas kernels: 0 us -> 159 us
  other arithmetic: 106 us -> 35.3 us
  local copies, waits for them, and re-layouts: 101 us -> 38.6 us
    ppermute x2 -> x13, waiting for transfers between devices: 555 us -> 250 us  [partner(): return lax.ppermute(block, axis, route)]
    dot_general x4, matrix products: 180 us -> 6.95 us  [the longest x2 4.27 us: on_device_paired(): jnp.einsum('qj,jxy->qxy', select, taken_rows, precision=exact)]
    dot_general x7, matrix products: 198 us -> 33.4 us  [matmul(): jnp.dot(first, second, precision=lax.Precision.HIGHEST, preferred_element...]
    pallas_call x0 -> x6, Pallas kernels: none -> 159 us  [the longest x5 107 us: schur_chunk(): pl.pallas_call(functools.partial(schur_kernel, chunk, rows_at_once), out_...]
    all_gather x4 -> x6, waiting for transfers between devices: 483 us -> 407 us  [the longest x5 326 us: on_device_paired(): gathered.append(lax.all_gather(piece, 'row', axis=0, tiled=True))]
    unnamed x13 -> x33, local copies, waits for them, and re-layouts: 48.8 us -> 0.66 us
    mul x3 -> x5, other arithmetic: 43.3 us -> 4.4 us  [the longest x2 2.77 us: on_device_paired(): lax.dynamic_slice(child, (at[i], 0, 0), (1, rows, BS))[0]]
    select_n x5 -> x8, other arithmetic: 55.2 us -> 19.5 us  [the longest x5 19.4 us: on_device_paired(): incoming = partner(jnp.where(side == 0, got, own), 'leaf', 0)]
  transfers between devices with their start and end apart: 7 -> 19, of which waited for: 7 -> 11; matrix products, arithmetic and copies ran while one was open for 8% -> 10% of each run, Pallas kernels for 0% -> 11%
where the time goes in v1:
time: 983 us; the launch traced here: 978 us
  waiting for transfers between devices  657 us (67%)
  Pallas kernels  159 us (16%)
  matrix products  40.4 us (4%)
  local copies, waits for them, and re-layouts  38.6 us (4%)
  other arithmetic  35.3 us (4%)
  between operations  24.5 us (2%)
  blocking collectives  16 us (2%)
    all_gather x5, waiting for transfers between devices, on_device_paired(): gathered.append(lax.all_gather(piece, 'row', axis=0, tiled=True))  326 us
    ppermute x13, waiting for transfers between devices, partner(): return lax.ppermute(block, axis, route)  250 us
    pallas_call x5, Pallas kernels, schur_chunk(): pl.pallas_call(functools.partial(schur_kernel, chunk, rows_at_once), out_...  107 us
    all_gather x1, waiting for transfers between devices, on_device_paired(): northern = lax.all_gather(trailing, 'row', axis=1)  80.7 us
    pallas_call x1, Pallas kernels, update(): pl.pallas_call(functools.partial(update_kernel, first_keep, panel_cols, r...  51.3 us
    dot_general x7, matrix products, matmul(): jnp.dot(first, second, precision=lax.Precision.HIGHEST, preferred_element...  33.4 us
  transfers between devices with their start and end apart: 19, of which 11 were waited for; matrix products, arithmetic and copies ran while one was open for 10% of the time, Pallas kernels for 11%

profile of v1, /device:TPU:0, one launch (start us, length us, event | category | flops | bytes accessed | tf_op | source)
XLA Modules:
  0.0 978.0 jit_solution(899060185449188400)
XLA Ops:
  6.5 5.0 fusion.63
  11.6 83.6 %all-gather.9.cloned.1.call-done.r_ref = f32[1024,8,128]{2,1,0:T(8,128)} async-done(((f32[256,8,128]{2,1,0:T(8,128)}), f32[1024,8,128]{2,1,0:T(8,128)}) %all-gather.9.cloned.1.call-update) | async-done | bytes 4194320 | tf_op jit(solution)/shard_map/all_gather | solution.py:320
  95.3 80.8 %all-gather.11.cloned.1.call-done.r_ref = f32[1024,8,128]{2,1,0:T(8,128)} async-done(((f32[256,8,128]{2,1,0:T(8,128)}), f32[1024,8,128]{2,1,0:T(8,128)}) %all-gather.11.cloned.1.call-update) | async-done | bytes 4194320 | tf_op jit(solution)/shard_map/all_gather | solution.py:320
  176.1 80.8 %all-gather.13.cloned.1.call-done.r_ref = f32[1024,8,128]{2,1,0:T(8,128)} async-done(((f32[256,8,128]{2,1,0:T(8,128)}), f32[1024,8,128]{2,1,0:T(8,128)}) %all-gather.13.cloned.1.call-update) | async-done | bytes 4194320 | tf_op jit(solution)/shard_map/all_gather | solution.py:320
  257.1 80.7 %all-gather.15.cloned.1.call-done.r_ref = f32[1024,8,128]{2,1,0:T(8,128)} async-done(((f32[256,8,128]{2,1,0:T(8,128)}), f32[1024,8,128]{2,1,0:T(8,128)}) %all-gather.15.cloned.1.call-update) | async-done | bytes 4194320 | tf_op jit(solution)/shard_map/all_gather | solution.py:320
  337.8 8.3 convolution_bitcast_fusion
  346.1 0.7 fusion.57
  347.0 0.6 copy.63
  348.0 6.6 convolution_bitcast_fusion.1
  354.6 3.1 fusion
  357.7 21.5 %schur_chunk.5 = (f32[4,1280,128]{2,1,0:T(8,128)}, f32[4,1280,128]{2,1,0:T(8,128)}) custom-call(s32[1]{0:T(128)} %bitcast.side_ref, s32[10,40]{1,0:T(8,128)} %bitcast.104, bf16[1280,1024]{1,0:T(8,128)(2,1)} %get-tuple-element.75.lh_ref, bf16[1280,1024]{1,0:T(8,128)(2,1)} %get-tuple-element.74.ll_ref, f32[1024,8,128]{2,1,0:T(8,128)} %all-gather.9.cloned.1.call-done.r_ref, ...), custom_call_target="tpu_custom_call" | custom-call | flops 8053063680 | bytes 19922944 | tf_op jit(solution)/shard_map/schur_chunk/pallas_call | solution.py:183
  379.2 0.5 collective-permute-start.1
  379.7 21.4 %schur_chunk.6 = (f32[4,1280,128]{2,1,0:T(8,128)}, f32[4,1280,128]{2,1,0:T(8,128)}) custom-call(s32[1]{0:T(128)} %bitcast.side_ref, s32[10,40]{1,0:T(8,128)} %bitcast.105, bf16[1280,1024]{1,0:T(8,128)(2,1)} %get-tuple-element.75.lh_ref, bf16[1280,1024]{1,0:T(8,128)(2,1)} %get-tuple-element.74.ll_ref, f32[1024,8,128]{2,1,0:T(8,128)} %all-gather.11.cloned.1.call-done.r_ref, ...), custom_call_target="tpu_custom_call" | custom-call | flops 8053063680 | bytes 19922944 | tf_op jit(solution)/shard_map/schur_chunk/pallas_call | solution.py:183
  401.2 21.6 %schur_chunk.7 = (f32[4,1280,128]{2,1,0:T(8,128)}, f32[4,1280,128]{2,1,0:T(8,128)}) custom-call(s32[1]{0:T(128)} %bitcast.side_ref, s32[10,40]{1,0:T(8,128)} %bitcast.106, bf16[1280,1024]{1,0:T(8,128)(2,1)} %get-tuple-element.75.lh_ref, bf16[1280,1024]{1,0:T(8,128)(2,1)} %get-tuple-element.74.ll_ref, f32[1024,8,128]{2,1,0:T(8,128)} %all-gather.13.cloned.1.call-done.r_ref, ...), custom_call_target="tpu_custom_call" | custom-call | flops 8053063680 | bytes 19922944 | tf_op jit(solution)/shard_map/schur_chunk/pallas_call | solution.py:183
  422.8 0.5 collective-permute-start.3
  423.3 21.4 %schur_chunk.8 = (f32[4,1280,128]{2,1,0:T(8,128)}, f32[4,1280,128]{2,1,0:T(8,128)}) custom-call(s32[1]{0:T(128)} %bitcast.side_ref, s32[10,40]{1,0:T(8,128)} %bitcast.107, bf16[1280,1024]{1,0:T(8,128)(2,1)} %get-tuple-element.75.lh_ref, bf16[1280,1024]{1,0:T(8,128)(2,1)} %get-tuple-element.74.ll_ref, f32[1024,8,128]{2,1,0:T(8,128)} %all-gather.15.cloned.1.call-done.r_ref, ...), custom_call_target="tpu_custom_call" | custom-call | flops 8053063680 | bytes 19922944 | tf_op jit(solution)/shard_map/schur_chunk/pallas_call | solution.py:183
  444.7 21.4 %schur_chunk.9 = (f32[4,1280,128]{2,1,0:T(8,128)}, f32[4,1280,128]{2,1,0:T(8,128)}) custom-call(s32[1]{0:T(128)} %bitcast.side_ref, s32[10,40]{1,0:T(8,128)} %bitcast.108, bf16[1280,1024]{1,0:T(8,128)(2,1)} %get-tuple-element.75.lh_ref, bf16[1280,1024]{1,0:T(8,128)(2,1)} %get-tuple-element.74.ll_ref, f32[1024,8,128]{2,1,0:T(8,128)} %all-gather.17.cloned.1.call-done.r_ref, ...), custom_call_target="tpu_custom_call" | custom-call | flops 8053063680 | bytes 19922944 | tf_op jit(solution)/shard_map/schur_chunk/pallas_call | solution.py:183
  466.6 4.4 broadcast_select_fusion.4
  471.1 1.5 collective-permute-start.6
  472.6 5.9 dynamic_update_slice.30
  478.5 2.7 broadcast_select_fusion.3
  481.8 4.7 broadcast_select_fusion.2
  486.5 1.5 collective-permute-start.8
  488.0 4.7 broadcast_select_fusion.1
  493.2 2.8 broadcast_select_fusion
  496.1 1.5 collective-permute-start.10
  497.6 0.6 iota_reduce_fusion.2
  498.3 1.1 iota_reduce_fusion.3
  500.3 30.8 %collective-permute-done.6 = f32[4,1280,128]{2,1,0:T(8,128)} collective-permute-done((f32[4,1280,128]{2,1,0:T(8,128)}, f32[4,1280,128]{2,1,0:T(8,128)}, u32[]{:S(2)}, u32[]{:S(2)}) %collective-permute-start.6) | collective-permute-done | bytes 2621472 | tf_op jit(solution)/shard_map/ppermute | solution.py:25
  531.1 3.0 dynamic_update_slice.35
  534.2 53.0 %collective-permute-done.7 = f32[4,1280,128]{2,1,0:T(8,128)S(1)} collective-permute-done((f32[4,1280,128]{2,1,0:T(8,128)}, f32[4,1280,128]{2,1,0:T(8,128)S(1)}, u32[]{:S(2)}, u32[]{:S(2)}) %collective-permute-start.7) | collective-permute-done | bytes 2621472 | tf_op jit(solution)/shard_map/ppermute | solution.py:25
  587.4 56.1 %collective-permute-done.8 = f32[4,1280,128]{2,1,0:T(8,128)} collective-permute-done((f32[4,1280,128]{2,1,0:T(8,128)}, f32[4,1280,128]{2,1,0:T(8,128)}, u32[]{:S(2)}, u32[]{:S(2)}) %collective-permute-start.8) | collective-permute-done | bytes 2621472 | tf_op jit(solution)/shard_map/ppermute | solution.py:25
  643.5 1.9 constant_dynamic-update-slice_fusion.2
  645.4 54.3 %collective-permute-done.9 = f32[4,1280,128]{2,1,0:T(8,128)} collective-permute-done((f32[4,1280,128]{2,1,0:T(8,128)}, f32[4,1280,128]{2,1,0:T(8,128)}, u32[]{:S(2)}, u32[]{:S(2)}) %collective-permute-start.9) | collective-permute-done | bytes 2621472 | tf_op jit(solution)/shard_map/ppermute | solution.py:25
  699.6 1.9 constant_dynamic-update-slice_fusion.1
  701.6 1.4 dynamic-slice_multiply_fusion.1
  703.0 51.9 %collective-permute-done.10 = f32[4,1280,128]{2,1,0:T(8,128)} collective-permute-done((f32[4,1280,128]{2,1,0:T(8,128)}, f32[4,1280,128]{2,1,0:T(8,128)}, u32[]{:S(2)}, u32[]{:S(2)}) %collective-permute-start.10) | collective-permute-done | bytes 2621472 | tf_op jit(solution)/shard_map/ppermute | solution.py:25
  754.9 1.9 constant_dynamic-update-slice_fusion.refs_8_.refs_9_.refs_10_.refs_11_.refs_12_.refs_13_.refs_14_.refs_15_
  756.9 2.0 fusion.20
  758.9 2.3 add_bitcast_fusion
  761.6 16.0 %all-gather = f32[4,2,128,128]{3,2,1,0:T(8,128)S(1)} all-gather(f32[1,2,128,128]{3,2,1,0:T(8,128)S(1)} %copy.40), channel_id=2, replica_groups=mesh['leaf'=4,'row'=4,'col'=2] {'row'}, dimensions={0}, use_global_device_ids=true | all-gather | bytes 655360 | tf_op jit(solution)/shard_map/all_gather | solution.py:378
  777.6 2.4 copy.42
  780.0 0.6 iota_reduce_fusion.1
  780.6 0.6 fusion.67
  783.9 0.7 iota_reduce_fusion
  784.6 0.6 fusion.65
  787.8 0.6 fusion.64
  789.7 0.6 fusion.66
  794.1 1.4 dynamic-slice_multiply_fusion.5
  796.4 1.2 fusion.6
  797.6 1.4 dynamic-slice_multiply_fusion.3
  799.9 1.4 add_multiply_fusion
  801.9 4.0 collective-permute-done.12
  806.0 1.8 copy.41
  807.8 2.1 reshape.211
  809.9 1.8 fusion.16
  811.7 1.9 fusion.26
  813.6 1.8 fusion.68
  815.4 2.1 convolution_subtract_fusion
  817.5 4.7 fusion.5
  822.2 5.8 copy.37
  828.0 10.9 %fusion.1 = (bf16[2048,512]{1,0:T(8,128)(2,1)}, bf16[2048,512]{1,0:T(8,128)(2,1)}) fusion(f32[512,512]{1,0:T(8,128)S(1)} %convolution_subtract_fusion, f32[64,8,16,128]{3,2,1,0:T(8,128)} %bitcast.94), kind=kOutput, calls=%fused_computation.6 | convolution fusion | flops 6446645248 | bytes 9437184 | tf_op jit(solution)/shard_map/dot_general | solution.py:34
  838.9 80.7 %all-gather.19.cloned.1.call-done.refs_18_.refs_19_.refs_20_.refs_21_ = f32[4,30,128,128]{3,2,1,0:T(8,128)} async-done(((f32[1,30,128,128]{3,2,1,0:T(8,128)}), f32[4,30,128,128]{3,2,1,0:T(8,128)}) %all-gather.19.cloned.1.call-update) | async-done | bytes 7864336 | tf_op jit(solution)/shard_map/all_gather | solution.py:380
  919.6 51.3 %front_update.1 = f32[2048,32,128]{2,1,0:T(8,128)} custom-call(s32[32]{0:T(128)} %copy-done.7, s32[32]{0:T(128)} %copy-done.9, s32[32]{0:T(128)} %copy-done.8, s32[32]{0:T(128)} %copy-done.10, s32[16]{0:T(128)} %copy-done.13, s32[16]{0:T(128)} %copy-done.15, s32[16]{0:T(128)} %copy-done.12, s32[16]{0:T(128)} %copy-done.14, ...), custom_call_target="tpu_custom_call" | custom-call | flops 25769803776 | bytes 83886080 | tf_op jit(solution)/shard_map/front_update/pallas_call | solution.py:266
  (97 shorter events, 6.3 us)
Async XLA Ops:
  6.5 340.4 %copy-start = (s32[4,2,40,40]{3,2,1,0:T(8,128)S(1)}, s32[4,2,40,40]{3,2,1,0:T(8,128)}, u32[]{:S(2)}) copy-start(s32[4,2,40,40]{3,2,1,0:T(8,128)} %param.9) | copy-start | bytes 153604
  6.5 88.6 %all-gather.9.cloned.1.call-start = ((), (), s32[]{:S(2)}) async-start(), calls=%async_computation | async-start | bytes 5242880 | tf_op jit(solution)/shard_map/all_gather | solution.py:320
  11.6 164.5 %all-gather.11.cloned.1.call-start = ((), (), s32[]{:S(2)}) async-start(), calls=%async_computation.1 | async-start | bytes 5242880 | tf_op jit(solution)/shard_map/all_gather | solution.py:320
  95.2 161.8 %all-gather.13.cloned.1.call-start = ((), (), s32[]{:S(2)}) async-start(), calls=%async_computation.2 | async-start | bytes 5242880 | tf_op jit(solution)/shard_map/all_gather | solution.py:320
  176.1 161.6 %all-gather.15.cloned.1.call-start = ((), (), s32[]{:S(2)}) async-start(), calls=%async_computation.3 | async-start | bytes 5242880 | tf_op jit(solution)/shard_map/all_gather | solution.py:320
  257.0 187.7 %all-gather.17.cloned.1.call-start = ((), (), s32[]{:S(2)}) async-start(), calls=%async_computation.4 | async-start | bytes 5242880 | tf_op jit(solution)/shard_map/all_gather | solution.py:320
  337.8 581.9 %all-gather.19.cloned.1.call-start = ((), (), s32[]{:S(2)}) async-start(), calls=%async_computation.5 | async-start | bytes 9830400 | tf_op jit(solution)/shard_map/all_gather | solution.py:380
  346.1 8.5 collective-permute-start
  379.2 87.4 %collective-permute-start.1 = (f32[4,1280,128]{2,1,0:T(8,128)}, f32[4,1280,128]{2,1,0:T(8,128)}, u32[]{:S(2)}, u32[]{:S(2)}) collective-permute-start(f32[4,1280,128]{2,1,0:T(8,128)} %get-tuple-element.35), channel_id=1, source_target_pairs={{0,1},{1,0},{2,3},{3,2},{4,5},{5,4},{6,7},{7,6},{8,9},{9,8},{10,11... | collective-permute-start | bytes 7864328 | tf_op jit(solution)/shard_map/ppermute | solution.py:25
  401.2 77.3 %collective-permute-start.2 = (f32[4,1280,128]{2,1,0:T(8,128)}, f32[4,1280,128]{2,1,0:T(8,128)S(1)}, u32[]{:S(2)}, u32[]{:S(2)}) collective-permute-start(f32[4,1280,128]{2,1,0:T(8,128)} %get-tuple-element.39), channel_id=1, source_target_pairs={{0,1},{1,0},{2,3},{3,2},{4,5},{5,4},{6,7},{7,6},{8,9},{9,8},{10,11... | collective-permute-start | bytes 7864328 | tf_op jit(solution)/shard_map/ppermute | solution.py:25
  422.8 59.0 %collective-permute-start.3 = (f32[4,1280,128]{2,1,0:T(8,128)}, f32[4,1280,128]{2,1,0:T(8,128)}, u32[]{:S(2)}, u32[]{:S(2)}) collective-permute-start(f32[4,1280,128]{2,1,0:T(8,128)} %get-tuple-element.43), channel_id=1, source_target_pairs={{0,1},{1,0},{2,3},{3,2},{4,5},{5,4},{6,7},{7,6},{8,9},{9,8},{10,11... | collective-permute-start | bytes 7864328 | tf_op jit(solution)/shard_map/ppermute | solution.py:25
  444.7 43.3 %collective-permute-start.4 = (f32[4,1280,128]{2,1,0:T(8,128)}, f32[4,1280,128]{2,1,0:T(8,128)}, u32[]{:S(2)}, u32[]{:S(2)}) collective-permute-start(f32[4,1280,128]{2,1,0:T(8,128)} %get-tuple-element.47), channel_id=1, source_target_pairs={{0,1},{1,0},{2,3},{3,2},{4,5},{5,4},{6,7},{7,6},{8,9},{9,8},{10,11... | collective-permute-start | bytes 7864328 | tf_op jit(solution)/shard_map/ppermute | solution.py:25
  466.1 27.1 %collective-permute-start.5 = (f32[4,1280,128]{2,1,0:T(8,128)}, f32[4,1280,128]{2,1,0:T(8,128)S(1)}, u32[]{:S(2)}, u32[]{:S(2)}) collective-permute-start(f32[4,1280,128]{2,1,0:T(8,128)} %get-tuple-element.50), channel_id=1, source_target_pairs={{0,1},{1,0},{2,3},{3,2},{4,5},{5,4},{6,7},{7,6},{8,9},{9,8},{10,11... | collective-permute-start | bytes 7864328 | tf_op jit(solution)/shard_map/ppermute | solution.py:25
  471.1 60.0 %collective-permute-start.6 = (f32[4,1280,128]{2,1,0:T(8,128)}, f32[4,1280,128]{2,1,0:T(8,128)}, u32[]{:S(2)}, u32[]{:S(2)}) collective-permute-start(f32[4,1280,128]{2,1,0:T(8,128)} %get-tuple-element.67), channel_id=1, source_target_pairs={{0,8},{8,0},{16,24},{24,16},{1,9},{9,1},{17,25},{25,17},{2,10},{10... | collective-permute-start | bytes 7864328 | tf_op jit(solution)/shard_map/ppermute | solution.py:25
  472.6 5.9 copy-start.6
  478.5 3.2 copy-start.5
  481.3 105.9 %collective-permute-start.7 = (f32[4,1280,128]{2,1,0:T(8,128)}, f32[4,1280,128]{2,1,0:T(8,128)S(1)}, u32[]{:S(2)}, u32[]{:S(2)}) collective-permute-start(f32[4,1280,128]{2,1,0:T(8,128)} %get-tuple-element.65), channel_id=1, source_target_pairs={{0,8},{8,0},{16,24},{24,16},{1,9},{9,1},{17,25},{25,17},{2,10},{10... | collective-permute-start | bytes 7864328 | tf_op jit(solution)/shard_map/ppermute | solution.py:25
  481.8 6.2 copy-start.4
  486.5 157.0 %collective-permute-start.8 = (f32[4,1280,128]{2,1,0:T(8,128)}, f32[4,1280,128]{2,1,0:T(8,128)}, u32[]{:S(2)}, u32[]{:S(2)}) collective-permute-start(f32[4,1280,128]{2,1,0:T(8,128)} %get-tuple-element.63), channel_id=1, source_target_pairs={{0,8},{8,0},{16,24},{24,16},{1,9},{9,1},{17,25},{25,17},{2,10},{10... | collective-permute-start | bytes 7864328 | tf_op jit(solution)/shard_map/ppermute | solution.py:25
  488.0 5.3 copy-start.3
  492.7 206.9 %collective-permute-start.9 = (f32[4,1280,128]{2,1,0:T(8,128)}, f32[4,1280,128]{2,1,0:T(8,128)}, u32[]{:S(2)}, u32[]{:S(2)}) collective-permute-start(f32[4,1280,128]{2,1,0:T(8,128)} %get-tuple-element.61), channel_id=1, source_target_pairs={{0,8},{8,0},{16,24},{24,16},{1,9},{9,1},{17,25},{25,17},{2,10},{10... | collective-permute-start | bytes 7864328 | tf_op jit(solution)/shard_map/ppermute | solution.py:25
  493.2 6.9 copy-start.11
  496.1 258.8 %collective-permute-start.10 = (f32[4,1280,128]{2,1,0:T(8,128)}, f32[4,1280,128]{2,1,0:T(8,128)}, u32[]{:S(2)}, u32[]{:S(2)}) collective-permute-start(f32[4,1280,128]{2,1,0:T(8,128)} %get-tuple-element.59), channel_id=1, source_target_pairs={{0,8},{8,0},{16,24},{24,16},{1,9},{9,1},{17,25},{25,17},{2,10},{10... | collective-permute-start | bytes 7864328 | tf_op jit(solution)/shard_map/ppermute | solution.py:25
  498.2 35.9 %copy-start.12 = (s32[16]{0:T(128)}, s32[16]{0:T(128)S(1)}, u32[]{:S(2)}) copy-start(s32[16]{0:T(128)S(1)} %get-tuple-element.32.second_row) | copy-start | bytes 196
  499.4 34.7 %copy-start.13 = (s32[16]{0:T(128)}, s32[16]{0:T(128)S(1)}, u32[]{:S(2)}) copy-start(s32[16]{0:T(128)S(1)} %get-tuple-element.31.first_row) | copy-start | bytes 196
  499.5 34.6 %copy-start.14 = (s32[16]{0:T(128)}, s32[16]{0:T(128)S(1)}, u32[]{:S(2)}) copy-start(s32[16]{0:T(128)S(1)} %convert_element_type.84.second_rowok) | copy-start | bytes 196
  499.7 34.4 %copy-start.15 = (s32[16]{0:T(128)}, s32[16]{0:T(128)S(1)}, u32[]{:S(2)}) copy-start(s32[16]{0:T(128)S(1)} %convert_element_type.83.first_rowok) | copy-start | bytes 196
  756.8 4.8 copy-start.2
  780.6 15.7 %copy-start.7 = (s32[32]{0:T(128)}, s32[32]{0:T(128)S(1)}, u32[]{:S(2)}) copy-start(s32[32]{0:T(128)S(1)} %get-tuple-element.29.first_col) | copy-start | bytes 388
  784.6 11.7 %copy-start.8 = (s32[32]{0:T(128)}, s32[32]{0:T(128)S(1)}, u32[]{:S(2)}) copy-start(s32[32]{0:T(128)S(1)} %get-tuple-element.30.second_col) | copy-start | bytes 388
  787.7 8.6 copy-start.9
  787.8 8.5 copy-start.10
  801.3 16.2 %collective-permute-start.11 = (f32[2,16,128,128]{3,1,2,0:T(8,128)S(1)}, f32[2,16,128,128]{3,1,2,0:T(8,128)}, u32[]{:S(2)}, u32[]{:S(2)}) collective-permute-start(f32[2,16,128,128]{3,1,2,0:T(8,128)S(1)} %bitcast.95), channel_id=1, source_target_pairs={{0,1},{1,0},{2,3},{3,2},{4,5},{5,4},{6,7},{7,6},{8,9},{9,8},{10,11... | collective-permute-start | bytes 6291464 | tf_op jit(solution)/shard_map/ppermute | solution.py:25
  801.4 4.5 collective-permute-start.12
  919.6 51.3 %copy-start.1 = (s32[4,2,40,40]{3,2,1,0:T(8,128)S(1)}, s32[4,2,40,40]{3,2,1,0:T(8,128)}, u32[]{:S(2)}) copy-start(s32[4,2,40,40]{3,2,1,0:T(8,128)} %param.9) | copy-start | bytes 153604
Sparse Core Ops, SparseCore 0:
  11.7 83.4 all-gather.8
  96.7 79.2 all-gather.10
  177.7 79.2 all-gather.12
  258.4 79.2 all-gather.14
  339.1 79.2 all-gather.16
  780.1 139.4 all-gather.18

commit v2 on v1

--- a/solution.py
+++ b/solution.py
@@ -145,54 +145,61 @@
     return dot(a_high, b_high) + (dot(a_high, b_low) + dot(a_low, b_high))
 
 
-def schur_kernel(chunk, rows_at_once, side_ref, mask_ref, lh_ref, ll_ref, r_ref, c_ref, own_ref, send_ref):
+def whole(shape):
+    return pl.BlockSpec(shape, lambda *_: (0,) * len(shape))
+
+
+def schur_kernel(chunk, side_ref, mask_ref, lh_ref, ll_ref, r_ref, c_ref, own_ref, send_ref, rh, rl):
     side = side_ref[0]
     rows, depth = lh_ref.shape
+    step = pl.program_id(0)
     r_flat = r_ref.reshape(depth * GROUP, BS)
     c_flat = c_ref.reshape(rows * GROUP, BS)
+
+    @pl.when(step == 0)
+    def _():
+        for pair in range(GROUP // 2):
+            right = jnp.concatenate(
+                [
+                    r_flat[pl.ds(q, depth, stride=GROUP), :]
+                    for q in (2 * pair + side, 2 * pair + 1 - side)
+                ],
+                axis=1,
+            )
+            rh[pair], rl[pair] = split_in_kernel(right)
+
     for pair in range(GROUP // 2):
-        q_own = 2 * pair + side
-        q_send = 2 * pair + 1 - side
-        right = jnp.concatenate(
-            [r_flat[pl.ds(q, depth, stride=GROUP), :] for q in (q_own, q_send)], axis=1
-        )
-        right_high, right_low = split_in_kernel(right)
-
-        def body(step, carry):
-            start = pl.multiple_of(step * rows_at_once, rows_at_once)
-            lines = pl.ds(start, rows_at_once)
-            product = dot3(lh_ref[lines, :], ll_ref[lines, :], right_high, right_low)
-            for place, (q, out_ref) in enumerate(((q_own, own_ref), (q_send, send_ref))):
-                c_part = c_flat[pl.ds(start * GROUP + q, rows_at_once, stride=GROUP), :]
-                value = c_part - product[:, place * BS : (place + 1) * BS]
-                for block in range(rows_at_once // BS):
-                    keep = mask_ref[step * (rows_at_once // BS) + block, chunk * GROUP + q]
-                    out_ref[pair, pl.ds(start + block * BS, BS), :] = value[
-                        block * BS : (block + 1) * BS
-                    ] * keep.astype(jnp.float32)
-            return carry
-
-        lax.fori_loop(0, rows // rows_at_once, body, 0)
-
-
-def schur_chunk(chunk, side, mask, left_high, left_low, right, cmat):
+        product = dot3(lh_ref[...], ll_ref[...], rh[pair], rl[pair])
+        for place, (q, out_ref) in enumerate(
+            ((2 * pair + side, own_ref), (2 * pair + 1 - side, send_ref))
+        ):
+            c_part = c_flat[pl.ds(q, rows, stride=GROUP), :]
+            value = c_part - product[:, place * BS : (place + 1) * BS]
+            for block in range(rows // BS):
+                keep = mask_ref[step * (rows // BS) + block, chunk * GROUP + q]
+                lines = slice(block * BS, (block + 1) * BS)
+                out_ref[pair, lines, :] = value[lines] * keep.astype(jnp.float32)
+
+
+def schur_chunk(chunk, inside, side, mask, left_high, left_low, right, cmat):
     rows, depth = left_high.shape
     half = jax.ShapeDtypeStruct((GROUP // 2, rows, BS), jnp.float32)
-    whole = lambda shape: pl.BlockSpec(shape, lambda i, *_: (0,) * len(shape))
-    rows_at_once = 2 * BS if rows % (2 * BS) == 0 else BS
+    part = 2 * BS if rows % (2 * BS) == 0 else BS
+    halves = pl.BlockSpec((GROUP // 2, part, BS), lambda i, *_: (0, i, 0))
     return pl.pallas_call(
-        functools.partial(schur_kernel, chunk, rows_at_once),
+        functools.partial(schur_kernel, chunk),
         out_shape=(half, half),
         grid_spec=pltpu.PrefetchScalarGridSpec(
             num_scalar_prefetch=2,
-            grid=(1,),
+            grid=(rows // part,),
             in_specs=[
-                whole((rows, depth)),
-                whole((rows, depth)),
-                whole((depth, GROUP, BS)),
-                pl.BlockSpec((rows, GROUP, BS), lambda i, *_: (0, chunk, 0)),
+                pl.BlockSpec((part, depth), lambda i, *_: (i, 0)),
+                pl.BlockSpec((part, depth), lambda i, *_: (i, 0)),
+                pl.BlockSpec((depth, GROUP, BS), lambda i, *_: (0, inside, 0)),
+                pl.BlockSpec((part, GROUP, BS), lambda i, *_: (i, chunk, 0)),
             ],
-            out_specs=[whole(half.shape), whole(half.shape)],
+            out_specs=[halves, halves],
+            scratch_shapes=[pltpu.VMEM((GROUP // 2, depth, 2 * BS), jnp.bfloat16)] * 2,
         ),
         compiler_params=pltpu.CompilerParams(vmem_limit_bytes=VMEM_LIMIT),
         cost_estimate=pl.CostEstimate(
@@ -204,7 +211,102 @@
     )(side, mask, left_high, left_low, right, cmat)
 
 
-def update_kernel(first_keep, panel_cols, row_step, first_col, first_colok, second_col, second_colok, first_row, first_rowok, second_row, second_rowok, *refs):
+def north_kernel(sizes, pieces, at0, ok0, at1, ok1, pivot_ref, first_ref, second_ref, diag_ref, *outs):
+    parent_cols = sum(sizes)
+    base = 0
+    for size, out_ref in zip(sizes, outs):
+        for piece in range(pieces):
+
+            def body(place, carry, base=base, piece=piece, out_ref=out_ref):
+                q = base + place
+                out_ref[piece, place] = (
+                    first_ref[piece, at0[q]] * ok0[q].astype(jnp.float32)
+                    + second_ref[piece, at1[q]] * ok1[q].astype(jnp.float32)
+                    + diag_ref[piece] * pivot_ref[piece * parent_cols + q].astype(jnp.float32)
+                )
+                return carry
+
+            lax.fori_loop(0, size, body, 0)
+        base += size
+
+
+def north_strips(sizes, scalars, on_pivot, first, second, diag):
+    pieces = first.shape[0]
+    shapes = [(pieces, size, BS, BS) for size in sizes]
+    return pl.pallas_call(
+        functools.partial(north_kernel, sizes, pieces),
+        out_shape=[jax.ShapeDtypeStruct(shape, jnp.float32) for shape in shapes],
+        grid_spec=pltpu.PrefetchScalarGridSpec(
+            num_scalar_prefetch=5,
+            grid=(1,),
+            in_specs=[whole(first.shape), whole(second.shape), whole(diag.shape)],
+            out_specs=[whole(shape) for shape in shapes],
+        ),
+        compiler_params=pltpu.CompilerParams(vmem_limit_bytes=VMEM_LIMIT),
+        name="north_strips",
+    )(*scalars, on_pivot, first, second, diag)
+
+
+def west_kernel(skip, col0, cok0, col1, cok1, row0, rok0, row1, rok1, first_ref, second_ref, out_ref):
+    q = pl.program_id(0)
+
+    def body(k, carry):
+        total = jnp.zeros((BS, BS), jnp.float32)
+        for ref, cok, row, rok in ((first_ref, cok0, row0, rok0), (second_ref, cok1, row1, rok1)):
+            lines = pl.ds(pl.multiple_of(row[k] * BS, BS), BS)
+            total = total + ref[0, lines, :] * (cok[q] * rok[k]).astype(jnp.float32)
+        below = jnp.where(k >= skip, 1.0, 0.0).astype(jnp.float32)
+        out_ref[0, pl.ds(pl.multiple_of(k * BS, BS), BS), :] = total * below
+        return carry
+
+    lax.fori_loop(0, out_ref.shape[1] // BS, body, 0)
+
+
+def west_columns(skip, panel_cols, parent_rows, scalars, first, second):
+    def slab(which):
+        return pl.BlockSpec((1, first.shape[1], BS), lambda q, *pre: (pre[which][q], 0, 0))
+
+    rows = parent_rows * BS
+    return pl.pallas_call(
+        functools.partial(west_kernel, skip),
+        out_shape=jax.ShapeDtypeStruct((panel_cols, rows, BS), jnp.float32),
+        grid_spec=pltpu.PrefetchScalarGridSpec(
+            num_scalar_prefetch=8,
+            grid=(panel_cols,),
+            in_specs=[slab(0), slab(2)],
+            out_specs=pl.BlockSpec((1, rows, BS), lambda q, *_: (q, 0, 0)),
+        ),
+        compiler_params=pltpu.CompilerParams(vmem_limit_bytes=VMEM_LIMIT),
+        name="west_columns",
+    )(*scalars, first, second)
+
+
+def scale_kernel(mine_ref, other_ref, near_ref, far_ref, high_ref, low_ref):
+    count = mine_ref.shape[0]
+    panel = jnp.concatenate([ref[i] for ref in (mine_ref, other_ref) for i in range(count)], axis=1)
+    middle = jnp.concatenate([ref[i] for ref in (near_ref, far_ref) for i in range(count)], axis=0)
+    scaled = dot3(*split_in_kernel(panel), *split_in_kernel(middle))
+    high_ref[...], low_ref[...] = split_in_kernel(scaled)
+
+
+def scale(mine, other, near, far):
+    count, rows, _ = mine.shape
+    width = near.shape[2]
+    part = 4 * BS if rows % (4 * BS) == 0 else BS
+    block = pl.BlockSpec((count, part, BS), lambda i: (0, i, 0))
+    out = pl.BlockSpec((part, width), lambda i: (i, 0))
+    return pl.pallas_call(
+        scale_kernel,
+        out_shape=[jax.ShapeDtypeStruct((rows, width), jnp.bfloat16)] * 2,
+        grid=(rows // part,),
+        in_specs=[block, block, whole(near.shape), whole(far.shape)],
+        out_specs=[out, out],
+        compiler_params=pltpu.CompilerParams(vmem_limit_bytes=VMEM_LIMIT),
+        name="scaled_panel",
+    )(mine, other, near, far)
+
+
+def update_kernel(first_keep, panel_cols, row_step, base, first_col, first_colok, second_col, second_colok, first_row, first_rowok, second_row, second_rowok, *refs):
     first = refs[:GROUP]
     second = refs[GROUP : 2 * GROUP]
     wh_ref, wl_ref = refs[2 * GROUP : 2 * GROUP + 2]
@@ -212,7 +314,7 @@
     out_ref = refs[-1]
     rows, width = wh_ref.shape
     out_flat = out_ref.reshape(rows * GROUP, BS)
-    group = pl.program_id(0)
+    group = base + pl.program_id(0)
     blocks = row_step // BS
     for pair in range(GROUP // 2):
         v_ref = v_refs[pair]
@@ -244,45 +346,52 @@
         lax.fori_loop(0, rows // row_step, body, 0)
 
 
-def update(first_keep, panel_cols, scalars, first, second, w_high, w_low, northern, parent_cols):
+def update(first_keep, panel_cols, scalars, first, second, w_high, w_low, northern, parent_cols, base, front):
     rows, width = w_high.shape
     child_rows = first.shape[1]
     pieces = northern.shape[0]
     row_step = 4 * BS if rows % (4 * BS) == 0 else BS
 
+    held = () if front is None else (front,)
+    inputs = (
+        [first] * GROUP + [second] * GROUP + [w_high, w_low] + [northern] * (GROUP // 2) + [*held]
+    )
+
     def slab(which, place):
         def at(g, *prefetched):
-            return prefetched[which][g * GROUP + place], 0, 0
+            return prefetched[which][(base + g) * GROUP + place], 0, 0
 
         return pl.BlockSpec((1, child_rows, BS), at)
 
     def north(pair):
         def at(g, *_):
-            return 0, jnp.maximum(g * (GROUP // 2) + pair - panel_cols // 2, 0), 0, 0
+            return 0, g * (GROUP // 2) + pair, 0, 0
 
         return pl.BlockSpec((pieces, 2, BS, BS), at)
 
-    whole = pl.BlockSpec((rows, width), lambda g, *_: (0, 0), pipeline_mode=pl.Buffered(1))
+    panel = pl.BlockSpec((rows, width), lambda g, *_: (0, 0), pipeline_mode=pl.Buffered(1))
     return pl.pallas_call(
-        functools.partial(update_kernel, first_keep, panel_cols, row_step),
+        functools.partial(update_kernel, first_keep, panel_cols, row_step, base),
         out_shape=jax.ShapeDtypeStruct((rows, parent_cols, BS), jnp.float32),
         grid_spec=pltpu.PrefetchScalarGridSpec(
             num_scalar_prefetch=8,
-            grid=(parent_cols // GROUP,),
+            grid=(northern.shape[1] // GROUP,),
             in_specs=[slab(0, i) for i in range(GROUP)]
             + [slab(2, i) for i in range(GROUP)]
-            + [whole, whole]
-            + [north(i) for i in range(GROUP // 2)],
-            out_specs=pl.BlockSpec((rows, GROUP, BS), lambda g, *_: (0, g, 0)),
+            + [panel, panel]
+            + [north(i) for i in range(GROUP // 2)]
+            + [pl.BlockSpec(memory_space=pl.ANY)] * len(held),
+            out_specs=pl.BlockSpec((rows, GROUP, BS), lambda g, *_: (0, base + g, 0)),
         ),
         compiler_params=pltpu.CompilerParams(vmem_limit_bytes=VMEM_LIMIT),
         cost_estimate=pl.CostEstimate(
-            flops=6 * rows * width * parent_cols * BS,
-            bytes_accessed=4 * (2 * child_rows + rows + width) * parent_cols * BS,
+            flops=6 * rows * width * northern.shape[1] * BS,
+            bytes_accessed=4 * (2 * child_rows + rows + width) * northern.shape[1] * BS,
             transcendentals=0,
         ),
         name="front_update",
-    )(*scalars, *([first] * GROUP), *([second] * GROUP), w_high, w_low, *([northern] * (GROUP // 2)))
+        input_output_aliases={8 + len(inputs) - 1: 0} if held else {},
+    )(*scalars, *inputs)
 
 
 def inverse_map(targets, count):
@@ -305,26 +414,31 @@
     width = PANB * BS
     panel_rows = PANB // row_count
     panel_cols = PANB // col_count
-    exact = lax.Precision.HIGHEST
 
     cmat = contribution.reshape(rows, child_cols, BS)
     right_local = panel_right.reshape(panel_right.shape[1], child_cols, BS)
     depth = right_local.shape[0] * row_count
-    chunks = child_cols // GROUP
-
-    gathered = []
-    for chunk in range(chunks):
+
+    def gather_right(chunk, *after):
         piece = right_local[:, chunk * GROUP : (chunk + 1) * GROUP]
-        if gathered:
-            piece, gathered[-1] = lax.optimization_barrier((piece, gathered[-1]))
-        gathered.append(lax.all_gather(piece, "row", axis=0, tiled=True))
+        if after:
+            piece = lax.optimization_barrier((piece, *after))[0]
+        if chunk % 2 == 0:
+            return lax.all_gather(piece, "row", axis=0, tiled=True)
+        whole_piece = lax.all_gather(piece[None], "row", axis=1, tiled=True)
+        return whole_piece.reshape(depth, GROUP, BS)
 
     local_left = panel_left.reshape(rows, panel_left.shape[4])
     local_depth = local_left.shape[1] // 2
     line = jnp.arange(2 * local_depth)[:, None]
     pick = 2 * jnp.arange(local_depth)[None, :]
-    kept = matmul(local_left, (line == pick + side).astype(jnp.float32))
-    given = matmul(local_left, (line == pick + 1 - side).astype(jnp.float32))
+    parted = [
+        jnp.dot(
+            local_left, (line == pick + offset).astype(jnp.float32), precision=lax.Precision.HIGH
+        )
+        for offset in (side, 1 - side)
+    ]
+    kept, given = parted
     taken = partner(given, "col", 0)
     left = jnp.where(
         side == 0,
@@ -335,16 +449,6 @@
 
     mask = block_masks[leaf_index, side].reshape(child_rows, row_count, blocks)[:, row_index]
     side_arg = side.astype(jnp.int32).reshape(1)
-    first = jnp.zeros((child_cols // 2, rows, BS), jnp.float32)
-    second = jnp.zeros((child_cols // 2, rows, BS), jnp.float32)
-    for chunk in range(chunks):
-        own, sent = schur_chunk(chunk, side_arg, mask, left_high, left_low, gathered[chunk], cmat)
-        got = partner(sent, "col", 0)
-        incoming = partner(jnp.where(side == 0, got, own), "leaf", 0)
-        at = chunk * (GROUP // 2)
-        first = lax.dynamic_update_slice(first, jnp.where(side == 0, own, got), (at, 0, 0))
-        second = lax.dynamic_update_slice(second, incoming, (at, 0, 0))
-
     maps = (index_maps[leaf_index, 0], index_maps[jnp.bitwise_xor(leaf_index, 1), 1])
     row_targets = [
         m.reshape(child_rows, row_count)[:, row_index].astype(jnp.int32) // row_count for m in maps
@@ -354,64 +458,108 @@
     ]
     cols = [inverse_map(t, parent_cols) for t in col_targets]
     lines = [inverse_map(t, parent_rows) for t in row_targets]
-    children = (first, second)
+    own_map = index_maps[leaf_index, side].reshape(child_rows, row_count)[:, row_index]
+    own_at, own_ok = inverse_map(own_map.astype(jnp.int32) // row_count, parent_rows)
+
+    def strip(block):
+        return jnp.stack(
+            [
+                lax.dynamic_slice(block, (0, own_at[i] * BS, 0), (GROUP // 2, BS, BS))
+                * own_ok[i].astype(jnp.float32)
+                for i in range(panel_rows)
+            ]
+        )
+
+    def crossed(own, sent):
+        got = partner(sent, "col", 0)
+        return jnp.where(side == 0, own, got), jnp.where(side == 0, got, own)
+
+    first = jnp.zeros((child_cols // 2, rows, BS), jnp.float32)
+    second = jnp.zeros((child_cols // 2, rows, BS), jnp.float32)
+    strips = ([], [])
+    chunks = child_cols // GROUP
+    gathered = [gather_right(chunk) for chunk in range(min(2, chunks))]
+    done = []
+    leaving_all = []
+    for chunk in range(chunks):
+        current = gathered[chunk]
+        after = (leaving_all[chunk - 1] + done[chunk - 1]) if chunk else [left_high, left_low]
+        if chunk + 2 < chunks:
+            gathered.append(gather_right(chunk + 2, current, *after))
+        elif chunk + 1 == chunks and chunk > 1:
+            after = leaving_all[chunk - 1] + done[chunk - 2] + [strips[1][chunk - 1]]
+            current = lax.optimization_barrier((current, *after))[0]
+        own, sent = schur_chunk(chunk, 0, side_arg, mask, left_high, left_low, current, cmat)
+        kept_strip, leaving_strip = crossed(strip(own), strip(sent))
+        strips[0].append(kept_strip)
+        strips[1].append(partner(leaving_strip, "leaf", 0))
+        kept, leaving = crossed(own, sent)
+        incoming = partner(leaving, "leaf", 0)
+        at = chunk * (GROUP // 2)
+        first = lax.dynamic_update_slice(first, kept, (at, 0, 0))
+        second = lax.dynamic_update_slice(second, incoming, (at, 0, 0))
+        leaving_all.append([leaving, leaving_strip])
+        done.append([incoming, strips[1][-1]])
 
     identity = jnp.eye(BS, dtype=jnp.float32)
     diag = pivot_diag.reshape(PANB, BS)
     col_blocks = jnp.arange(parent_cols) * col_count + side
-
-    north_local = []
-    for piece in range(panel_rows):
-        strip = jnp.zeros((parent_cols, BS, BS), jnp.float32)
-        for child, (at, ok), target in zip(children, lines, col_targets):
-            taken_rows = lax.dynamic_slice(
-                child, (0, at[piece] * BS, 0), (child.shape[0], BS, BS)
-            ) * ok[piece].astype(jnp.float32)
-            select = (target[None, :] == jnp.arange(parent_cols)[:, None]).astype(jnp.float32)
-            strip = strip + jnp.einsum("qj,jxy->qxy", select, taken_rows, precision=exact)
-        row_block = piece * row_count + row_index
-        on_pivot = (col_blocks == row_block).astype(jnp.float32)
-        strip = strip + on_pivot[:, None, None] * (diag[row_block][:, None] * identity)[None]
-        north_local.append(strip)
-    north_local = jnp.stack(north_local)
-
-    corner = lax.all_gather(north_local[:, :panel_cols], "row", axis=1)
-    trailing, corner = lax.optimization_barrier((north_local[:, panel_cols:], corner))
-    northern = lax.all_gather(trailing, "row", axis=1)
-    northern = northern.reshape(PANB, parent_cols - panel_cols, BS, BS)
-
-    def both_sides(mine):
-        other = partner(mine, "col", 0)
-        return jnp.where(side == 0, jnp.stack([mine, other]), jnp.stack([other, mine]))
-
-    corner = corner.reshape(PANB, panel_cols, BS, BS)
-    pivot = jnp.transpose(both_sides(corner), (1, 3, 2, 0, 4)).reshape(width, width)
-
-    west = jnp.zeros((panel_cols, parent_rows, BS, BS), jnp.float32)
-    for child, (at, ok), target in zip(children, cols, row_targets):
-        slabs = jnp.stack(
-            [
-                lax.dynamic_slice(child, (at[i], 0, 0), (1, rows, BS))[0]
-                * ok[i].astype(jnp.float32)
-                for i in range(panel_cols)
-            ]
-        ).reshape(panel_cols, child_rows, BS, BS)
-        select = (target[None, :] == jnp.arange(parent_rows)[:, None]).astype(jnp.float32)
-        west = west + jnp.einsum("pk,qkxy->qpxy", select, slabs, precision=exact)
-    below = (jnp.arange(parent_rows) >= panel_rows).astype(jnp.float32)
-    west = west * below[None, :, None, None]
-    western = jnp.transpose(both_sides(west), (2, 3, 1, 0, 4)).reshape(parent_rows * BS, width)
-
+    panel_blocks = jnp.arange(panel_rows) * row_count + row_index
+    diag_blocks = diag[panel_blocks][:, :, None] * identity[None]
+    on_pivot = (panel_blocks[:, None] == col_blocks[None, :]).astype(jnp.int32).reshape(-1)
+    groups = parent_cols // GROUP
+    widths = (1, groups - 2, 1) if groups > 2 else (1,) * groups
+    north = north_strips(
+        tuple(w * GROUP for w in widths),
+        (*cols[0], *cols[1]),
+        on_pivot,
+        jnp.concatenate(strips[0], axis=1),
+        jnp.concatenate(strips[1], axis=1),
+        diag_blocks,
+    )
+    northern = []
+    for piece in north:
+        if northern:
+            before = [incoming[0] for incoming in done[-2:-1]] if len(northern) == 1 else []
+            piece = lax.optimization_barrier((piece, northern[-1], *before))[0]
+        northern.append(lax.all_gather(piece, "row", axis=1))
+    northern = [piece.reshape(PANB, -1, BS, BS) for piece in northern]
+
+    corner = northern[0][:, :panel_cols]
+    far_corner = partner(corner, "col", 0)
+    both = jnp.where(
+        side == 0, jnp.stack([corner, far_corner]), jnp.stack([far_corner, corner])
+    )
+    pivot = jnp.transpose(both, (1, 3, 2, 0, 4)).reshape(width, width)
     inverse = jnp.diag(1.0 / pivot_diag)
     for sweep in range(NS_STEPS):
         inverse = 2.0 * inverse - matmul(matmul(inverse, pivot), inverse)
-    scaled_high, scaled_low = split(matmul(western, inverse))
+    bands = inverse.reshape(panel_cols, 2, BS, width)
+    near = jnp.where(side == 0, bands[:, 0], bands[:, 1])
+    far = jnp.where(side == 0, bands[:, 1], bands[:, 0])
 
     scalars = (*cols[0], *cols[1], *lines[0], *lines[1])
-    result = update(
-        panel_rows, panel_cols, scalars, first, second, scaled_high, scaled_low, northern, parent_cols
-    )
-    return result.reshape(1, parent_rows, 1, BS, parent_cols, 1, BS)
+    west = west_columns(panel_rows, panel_cols, parent_rows, scalars, first, second)
+    scaled_high, scaled_low = scale(west, partner(west, "col", 0), near, far)
+
+    front = None
+    base = 0
+    for size, piece in zip(widths, northern):
+        front = update(
+            panel_rows,
+            panel_cols,
+            scalars,
+            first,
+            second,
+            scaled_high,
+            scaled_low,
+            piece,
+            parent_cols,
+            base,
+            front,
+        )
+        base += size
+    return front.reshape(1, parent_rows, 1, BS, parent_cols, 1, BS)
 
 
 def on_device(contribution, *others):

time: 983 us -> 702 us (0.71)
  waiting for transfers between devices: 657 us -> 385 us
  matrix products: 40.4 us -> 19.5 us
  other arithmetic: 35.3 us -> 51.8 us
  blocking collectives: 16 us -> 0 us
  between operations: 24.5 us -> 14.1 us
    all_gather x6 -> x8, waiting for transfers between devices: 407 us -> 163 us  [the longest x2 96 us: gather_right(): whole_piece = lax.all_gather(piece[None], 'row', axis=1, tiled=True)]
    ppermute x13 -> x23, waiting for transfers between devices: 250 us -> 222 us  [partner(): return lax.ppermute(block, axis, route)]
    dot_general x7 -> x4, matrix products: 33.4 us -> 7.42 us  [matmul(): jnp.dot(first, second, precision=lax.Precision.HIGHEST, preferred_element...]
    pallas_call x1 -> x3, Pallas kernels: 51.3 us -> 70.9 us  [update(): pl.pallas_call(functools.partial(update_kernel, first_keep, panel_cols, r...]
    all_gather x1 -> x0, blocking collectives: 16 us -> none  [on_device_paired(): corner = lax.all_gather(north_local[:, :panel_cols], 'row', axis=1)]
    pallas_call x5 -> x8, Pallas kernels: 107 us -> 93.8 us  [the longest x5 78.5 us: schur_chunk(): pl.pallas_call(functools.partial(schur_kernel, chunk), out_shape=(half, h...]
    dynamic_update_slice x5, local copies, waits for them, and re-layouts: 8.92 us -> 19.7 us  [on_device_paired(): second = lax.dynamic_update_slice(second, incoming, (at, 0, 0))]
    select_n x5 -> x8, other arithmetic: 19.4 us -> 23.2 us  [the longest x6 22.1 us: crossed(): return (jnp.where(side == 0, own, got), jnp.where(side == 0, got, own))]
  transfers between devices with their start and end apart: 19 -> 31, of which waited for: 11 -> 14; matrix products, arithmetic and copies ran while one was open for 10% -> 15% of each run, Pallas kernels for 11% -> 18%
where the time goes in v2:
time: 702 us; the launch traced here: 693 us
  waiting for transfers between devices  385 us (55%)
  Pallas kernels  165 us (24%)
  other arithmetic  51.8 us (7%)
  local copies, waits for them, and re-layouts  43 us (6%)
  matrix products  19.5 us (3%)
  starting transfers between devices  15 us (2%)
  between operations  14.1 us (2%)
    ppermute x23, waiting for transfers between devices, partner(): return lax.ppermute(block, axis, route)  222 us
    all_gather x2, waiting for transfers between devices, gather_right(): whole_piece = lax.all_gather(piece[None], 'row', axis=1, tiled=True)  96 us
    pallas_call x5, Pallas kernels, schur_chunk(): pl.pallas_call(functools.partial(schur_kernel, chunk), out_shape=(half, h...  78.5 us
    pallas_call x3, Pallas kernels, update(): pl.pallas_call(functools.partial(update_kernel, first_keep, panel_cols, r...  70.9 us
    all_gather x3, waiting for transfers between devices, gather_right(): return lax.all_gather(piece, 'row', axis=0, tiled=True)  66.5 us
    select_n x6, other arithmetic, crossed(): return (jnp.where(side == 0, own, got), jnp.where(side == 0, got, own))  22.1 us
    dynamic_update_slice x5, local copies, waits for them, and re-layouts, on_device_paired(): second = lax.dynamic_update_slice(second, incoming, (at, 0, 0))  19.7 us
    ppermute x23, starting transfers between devices, partner(): return lax.ppermute(block, axis, route)  14.5 us
  transfers between devices with their start and end apart: 31, of which 14 were waited for; matrix products, arithmetic and copies ran while one was open for 15% of the time, Pallas kernels for 18%

profile of v2, /device:TPU:0, one launch (start us, length us, event | category | flops | bytes accessed | tf_op | source)
XLA Modules:
  0.0 693.1 jit_solution(12649252736375264202)
XLA Ops:
  6.5 5.0 fusion.36
  12.4 6.9 convolution_bitcast_fusion
  20.3 5.2 convolution_bitcast_fusion.1
  25.5 3.1 fusion
  28.7 66.5 %all-gather.14.cloned.1.call-done.r_ref = f32[1024,8,128]{2,1,0:T(8,128)} async-done(((f32[256,8,128]{2,1,0:T(8,128)}), f32[1024,8,128]{2,1,0:T(8,128)}) %all-gather.14.cloned.1.call-update) | async-done | bytes 4194320 | tf_op jit(solution)/shard_map/all_gather | solution.py:427
  95.2 15.8 %schur_chunk.5 = (f32[4,1280,128]{2,1,0:T(8,128)}, f32[4,1280,128]{2,1,0:T(8,128)}) custom-call(s32[1]{0:T(128)} %bitcast.side_ref, s32[10,40]{1,0:T(8,128)} %bitcast.101, bf16[1280,1024]{1,0:T(8,128)(2,1)} %get-tuple-element.87.lh_ref, bf16[1280,1024]{1,0:T(8,128)(2,1)} %get-tuple-element.86.ll_ref, f32[1024,8,128]{2,1,0:T(8,128)} %all-gather.14.cloned.1.call-done.r_ref, ...), custom_call_target="tpu_custom_call" | custom-call | flops 8053063680 | bytes 19922944 | tf_op jit(solution)/shard_map/schur_chunk/pallas_call | solution.py:189
  111.0 5.1 collective-permute-done.1
  116.1 3.9 broadcast_select_fusion.4
  120.0 1.5 collective-permute-start.5
  123.8 1.0 multiply_bitcast_fusion.4
  124.8 1.5 collective-permute-done.4
  126.4 1.7 fusion.19
  128.5 47.5 %all-gather.20.cloned.1.call-done.r_ref = f32[1024,8,128]{2,1,0:T(8,128)} async-done(((f32[256,8,128]{2,1,0:T(8,128)}), f32[1024,8,128]{2,1,0:T(8,128)}) %all-gather.20.cloned.1.call-update) | async-done | bytes 4194320 | tf_op jit(solution)/shard_map/all_gather | solution.py:428
  176.1 8.7 %collective-permute-done.6 = f32[1,4,128,128]{3,2,1,0:T(8,128)S(1)} collective-permute-done((f32[1,4,128,128]{3,2,1,0:T(8,128)S(1)}, f32[1,4,128,128]{3,2,1,0:T(8,128)S(1)}, u32[]{:S(2)}, u32[]{:S(2)}) %collective-permute-start.6) | collective-permute-done | bytes 262176 | tf_op jit(solution)/shard_map/ppermute | solution.py:25
  185.1 15.7 %schur_chunk.6 = (f32[4,1280,128]{2,1,0:T(8,128)}, f32[4,1280,128]{2,1,0:T(8,128)}) custom-call(s32[1]{0:T(128)} %bitcast.side_ref, s32[10,40]{1,0:T(8,128)} %bitcast.102, bf16[1280,1024]{1,0:T(8,128)(2,1)} %get-tuple-element.87.lh_ref, bf16[1280,1024]{1,0:T(8,128)(2,1)} %get-tuple-element.86.ll_ref, f32[1024,8,128]{2,1,0:T(8,128)} %all-gather.20.cloned.1.call-done.r_ref, ...), custom_call_target="tpu_custom_call" | custom-call | flops 8053063680 | bytes 19922944 | tf_op jit(solution)/shard_map/schur_chunk/pallas_call | solution.py:189
  200.8 5.9 dynamic_update_slice.30
  206.7 1.9 broadcast_select_fusion.3
  208.6 1.6 collective-permute-start.9
  210.2 1.0 multiply_bitcast_fusion.3
  211.5 1.3 collective-permute-done.8
  214.0 59.5 %collective-permute-done.10 = f32[1,4,128,128]{3,2,1,0:T(8,128)S(1)} collective-permute-done((f32[1,4,128,128]{3,2,1,0:T(8,128)S(1)}, f32[1,4,128,128]{3,2,1,0:T(8,128)S(1)}, u32[]{:S(2)}, u32[]{:S(2)}) %collective-permute-start.10) | collective-permute-done | bytes 262176 | tf_op jit(solution)/shard_map/ppermute | solution.py:25
  273.6 15.6 %schur_chunk.7 = (f32[4,1280,128]{2,1,0:T(8,128)}, f32[4,1280,128]{2,1,0:T(8,128)}) custom-call(s32[1]{0:T(128)} %bitcast.side_ref, s32[10,40]{1,0:T(8,128)} %bitcast.103, bf16[1280,1024]{1,0:T(8,128)(2,1)} %get-tuple-element.87.lh_ref, bf16[1280,1024]{1,0:T(8,128)(2,1)} %get-tuple-element.86.ll_ref, f32[1024,8,128]{2,1,0:T(8,128)} %all-gather.16.cloned.1.call-done.r_ref, ...), custom_call_target="tpu_custom_call" | custom-call | flops 8053063680 | bytes 19922944 | tf_op jit(solution)/shard_map/schur_chunk/pallas_call | solution.py:189
  289.2 48.5 %all-gather.22.cloned.1.call-done.r_ref = f32[1024,8,128]{2,1,0:T(8,128)} async-done(((f32[256,8,128]{2,1,0:T(8,128)}), f32[1024,8,128]{2,1,0:T(8,128)}) %all-gather.22.cloned.1.call-update) | async-done | bytes 4194320 | tf_op jit(solution)/shard_map/all_gather | solution.py:428
  337.7 15.7 %schur_chunk.8 = (f32[4,1280,128]{2,1,0:T(8,128)}, f32[4,1280,128]{2,1,0:T(8,128)}) custom-call(s32[1]{0:T(128)} %bitcast.side_ref, s32[10,40]{1,0:T(8,128)} %bitcast.104, bf16[1280,1024]{1,0:T(8,128)(2,1)} %get-tuple-element.87.lh_ref, bf16[1280,1024]{1,0:T(8,128)(2,1)} %get-tuple-element.86.ll_ref, f32[1024,8,128]{2,1,0:T(8,128)} %all-gather.22.cloned.1.call-done.r_ref, ...), custom_call_target="tpu_custom_call" | custom-call | flops 8053063680 | bytes 19922944 | tf_op jit(solution)/shard_map/schur_chunk/pallas_call | solution.py:189
  353.5 1.5 copy-done.5
  355.0 5.4 broadcast_select_fusion.1
  360.5 1.6 collective-permute-start.12
  363.9 1.0 multiply_bitcast_fusion.1
  365.8 1.0 multiply_bitcast_fusion.2
  367.3 1.7 fusion.16
  370.2 1.6 collective-permute-start.15
  371.8 4.6 broadcast_select_fusion.2
  376.4 49.6 %collective-permute-done.14 = f32[1,4,128,128]{3,2,1,0:T(8,128)S(1)} collective-permute-done((f32[1,4,128,128]{3,2,1,0:T(8,128)S(1)}, f32[1,4,128,128]{3,2,1,0:T(8,128)S(1)}, u32[]{:S(2)}, u32[]{:S(2)}) %collective-permute-start.14) | collective-permute-done | bytes 262176 | tf_op jit(solution)/shard_map/ppermute | solution.py:25
  426.7 4.6 collective-permute-done.15
  431.3 15.6 %schur_chunk.9 = (f32[4,1280,128]{2,1,0:T(8,128)}, f32[4,1280,128]{2,1,0:T(8,128)}) custom-call(s32[1]{0:T(128)} %bitcast.side_ref, s32[10,40]{1,0:T(8,128)} %bitcast.105, bf16[1280,1024]{1,0:T(8,128)(2,1)} %get-tuple-element.87.lh_ref, bf16[1280,1024]{1,0:T(8,128)(2,1)} %get-tuple-element.86.ll_ref, f32[1024,8,128]{2,1,0:T(8,128)} %all-gather.18.cloned.1.call-done.r_ref, ...), custom_call_target="tpu_custom_call" | custom-call | flops 8053063680 | bytes 19922944 | tf_op jit(solution)/shard_map/schur_chunk/pallas_call | solution.py:189
  446.9 1.0 multiply_bitcast_fusion
  450.3 1.7 bitcast_select_fusion
  452.0 1.5 collective-permute-start.21
  455.0 1.8 constant_dynamic-update-slice_fusion.1
  456.8 3.9 collective-permute-done.21
  461.4 4.4 north_strips.1
  465.9 1.6 collective-permute-start.17
  467.5 57.2 %collective-permute-done.17 = f32[4,1280,128]{2,1,0:T(8,128)} collective-permute-done((f32[4,1280,128]{2,1,0:T(8,128)}, f32[4,1280,128]{2,1,0:T(8,128)}, u32[]{:S(2)}, u32[]{:S(2)}) %collective-permute-start.17) | collective-permute-done | bytes 2621472 | tf_op jit(solution)/shard_map/ppermute | solution.py:25
  524.8 4.5 broadcast_select_fusion
  529.4 1.5 collective-permute-start.18
  532.6 9.0 %iota_reduce_fusion.3 = (pred[16]{0:T(512)(128)(4,1)}, s32[16]{0:T(128)}) fusion(s32[10]{0:T(128)S(1)} %get-tuple-element.108), kind=kLoop, calls=%fused_computation.83 | loop fusion | flops 1168 | bytes 120 | tf_op jit(solution)/shard_map/inverse_map/reduce | solution.py:399
  542.3 7.7 %dynamic_update_slice.35 = f32[20,1280,128]{2,1,0:T(8,128)} pad(f32[4,1280,128]{2,1,0:T(8,128)} %collective-permute-done.5, f32[]{:T(128)} %constant.94.clone.1), padding=0_16x0_0x0_0 | pad | bytes 15728644 | tf_op jit(solution)/shard_map/dynamic_update_slice | solution.py:500
  550.0 3.4 constant_dynamic-update-slice_fusion.8
  553.4 3.5 constant_dynamic-update-slice_fusion.7
  556.9 3.4 constant_dynamic-update-slice_fusion.6
  560.3 26.9 %collective-permute-done.18 = f32[4,1280,128]{2,1,0:T(8,128)S(1)} collective-permute-done((f32[4,1280,128]{2,1,0:T(8,128)}, f32[4,1280,128]{2,1,0:T(8,128)S(1)}, u32[]{:S(2)}, u32[]{:S(2)}) %collective-permute-start.18) | collective-permute-done | bytes 2621472 | tf_op jit(solution)/shard_map/ppermute | solution.py:25
  587.2 1.7 constant_dynamic-update-slice_fusion.5.second_ref.refs_8_.refs_9_.refs_10_.refs_11_.refs_12_.refs_13_.refs_14_.refs_15_
  588.8 3.7 west_columns.1.mine_ref
  592.5 1.1 slice_bitcast_fusion.2
  594.3 3.2 collective-permute-done.22
  599.2 1.9 fusion.3
  601.0 1.9 fusion.5
  602.9 1.8 fusion.37
  604.8 1.8 convolution_subtract_fusion
  606.6 1.1 select_bitcast_fusion
  607.8 7.3 %scaled_panel.1 = (bf16[2048,512]{1,0:T(8,128)(2,1)}, bf16[2048,512]{1,0:T(8,128)(2,1)}) custom-call(f32[2,2048,128]{2,1,0:T(8,128)} %west_columns.1.mine_ref, f32[2,2048,128]{2,1,0:T(8,128)} %collective-permute-done.19.other_ref, f32[2,128,512]{2,1,0:T(8,128)} %get-tuple-element.101.near_ref, f32[2,128,512]{2,1,0:T(8,128)} %get-tuple-element.100.far_ref), custom_call_target="tpu_custom_call" | custom-call | tf_op jit(solution)/shard_map/scaled_panel/pallas_call | solution.py:298
  615.0 19.7 %front_update.3.refs_22_ = f32[2048,32,128]{2,1,0:T(8,128)} custom-call(s32[32]{0:T(128)} %get-tuple-element.31.col0.at0.first_col, s32[32]{0:T(128)} %convert_element_type.44.cok0.ok0.first_colok, s32[32]{0:T(128)} %get-tuple-element.32.col1.at1.second_col, s32[32]{0:T(128)} %convert_element_type.45.cok1.ok1.second_colok, ...), custom_call_target="tpu_custom_call" | custom-call | flops 6442450944 | bytes 20971520 | tf_op jit(solution)/shard_map/front_update/pallas_call | solution.py:373
  634.8 31.5 %front_update.4.refs_22_ = f32[2048,32,128]{2,1,0:T(8,128)} custom-call(s32[32]{0:T(128)} %get-tuple-element.31.col0.at0.first_col, s32[32]{0:T(128)} %convert_element_type.44.cok0.ok0.first_colok, s32[32]{0:T(128)} %get-tuple-element.32.col1.at1.second_col, s32[32]{0:T(128)} %convert_element_type.45.cok1.ok1.second_colok, ...), custom_call_target="tpu_custom_call", output_to_operand_aliasing={{}: (30, {})} | custom-call | flops 12884901888 | bytes 41943040 | tf_op jit(solution)/shard_map/front_update/pallas_call | solution.py:373
  666.3 19.8 %front_update.5 = f32[2048,32,128]{2,1,0:T(8,128)} custom-call(s32[32]{0:T(128)} %get-tuple-element.31.col0.at0.first_col, s32[32]{0:T(128)} %convert_element_type.44.cok0.ok0.first_colok, s32[32]{0:T(128)} %get-tuple-element.32.col1.at1.second_col, s32[32]{0:T(128)} %convert_element_type.45.cok1.ok1.second_colok, ...), custom_call_target="tpu_custom_call", output_to_operand_aliasing={{}: (30, {})} | custom-call | flops 6442450944 | bytes 20971520 | tf_op jit(solution)/shard_map/front_update/pallas_call | solution.py:373
  (111 shorter events, 21.0 us)
Async XLA Ops:
  6.5 13.2 %copy-start = (s32[4,2,40,40]{3,2,1,0:T(8,128)S(1)}, s32[4,2,40,40]{3,2,1,0:T(8,128)}, u32[]{:S(2)}) copy-start(s32[4,2,40,40]{3,2,1,0:T(8,128)} %param.9) | copy-start | bytes 153604
  6.5 88.6 %all-gather.14.cloned.1.call-start = ((), (), s32[]{:S(2)}) async-start(), calls=%async_computation | async-start | bytes 5242880 | tf_op jit(solution)/shard_map/all_gather | solution.py:427
  11.5 164.5 %all-gather.20.cloned.1.call-start = ((), (), s32[]{:S(2)}) async-start(), calls=%async_computation.3 | async-start | bytes 5242880 | tf_op jit(solution)/shard_map/all_gather | solution.py:428
  12.3 261.2 %all-gather.16.cloned.1.call-start = ((), (), s32[]{:S(2)}) async-start(), calls=%async_computation.1 | async-start | bytes 5242880 | tf_op jit(solution)/shard_map/all_gather | solution.py:427
  19.3 6.3 collective-permute-start
  95.2 242.5 %all-gather.22.cloned.1.call-start = ((), (), s32[]{:S(2)}) async-start(), calls=%async_computation.4 | async-start | bytes 5242880 | tf_op jit(solution)/shard_map/all_gather | solution.py:428
  111.0 5.1 collective-permute-start.1
  120.0 64.7 %collective-permute-start.5 = (f32[4,1280,128]{2,1,0:T(8,128)}, f32[4,1280,128]{2,1,0:T(8,128)}, u32[]{:S(2)}, u32[]{:S(2)}) collective-permute-start(f32[4,1280,128]{2,1,0:T(8,128)} %get-tuple-element.84), channel_id=1, source_target_pairs={{0,8},{8,0},{16,24},{24,16},{1,9},{9,1},{17,25},{25,17},{2,10},{10... | collective-permute-start | bytes 7864328 | tf_op jit(solution)/shard_map/ppermute | solution.py:25
  124.7 1.6 collective-permute-start.4
  128.0 56.7 %collective-permute-start.6 = (f32[1,4,128,128]{3,2,1,0:T(8,128)S(1)}, f32[1,4,128,128]{3,2,1,0:T(8,128)S(1)}, u32[]{:S(2)}, u32[]{:S(2)}) collective-permute-start(f32[1,4,128,128]{3,2,1,0:T(8,128)S(1)} %get-tuple-element.97), channel_id=1, source_target_pairs={{0,8},{8,0},{16,24},{24,16},{1,9},{9,1},{17,25},{25,17},{2,10},{10... | collective-permute-start | bytes 786440 | tf_op jit(solution)/shard_map/ppermute | solution.py:25
  184.8 246.5 %all-gather.18.cloned.1.call-start = ((), (), s32[]{:S(2)}) async-start(), calls=%async_computation.2 | async-start | bytes 5242880 | tf_op jit(solution)/shard_map/all_gather | solution.py:427
  200.8 5.9 collective-permute-start.2
  200.8 5.9 copy-start.4
  208.6 64.9 %collective-permute-start.9 = (f32[4,1280,128]{2,1,0:T(8,128)S(1)}, f32[4,1280,128]{2,1,0:T(8,128)}, u32[]{:S(2)}, u32[]{:S(2)}) collective-permute-start(f32[4,1280,128]{2,1,0:T(8,128)S(1)} %get-tuple-element.77), channel_id=1, source_target_pairs={{0,8},{8,0},{16,24},{24,16},{1,9},{9,1},{17,25},{25,17},{2,10},{10... | collective-permute-start | bytes 7864328 | tf_op jit(solution)/shard_map/ppermute | solution.py:25
  211.2 1.6 collective-permute-start.8
  213.6 60.0 %collective-permute-start.10 = (f32[1,4,128,128]{3,2,1,0:T(8,128)S(1)}, f32[1,4,128,128]{3,2,1,0:T(8,128)S(1)}, u32[]{:S(2)}, u32[]{:S(2)}) collective-permute-start(f32[1,4,128,128]{3,2,1,0:T(8,128)S(1)} %get-tuple-element.95), channel_id=1, source_target_pairs={{0,8},{8,0},{16,24},{24,16},{1,9},{9,1},{17,25},{25,17},{2,10},{10... | collective-permute-start | bytes 786440 | tf_op jit(solution)/shard_map/ppermute | solution.py:25
  273.5 319.0 %all-gather.24.cloned.1.call-start = ((), (), s32[]{:S(2)}) async-start(), calls=%async_computation.5 | async-start | bytes 2621440 | tf_op jit(solution)/shard_map/all_gather | solution.py:525
  289.2 64.3 %collective-permute-start.3 = (f32[4,1280,128]{2,1,0:T(8,128)}, f32[4,1280,128]{2,1,0:T(8,128)S(1)}, u32[]{:S(2)}, u32[]{:S(2)}) collective-permute-start(f32[4,1280,128]{2,1,0:T(8,128)} %get-tuple-element.41), channel_id=1, source_target_pairs={{0,1},{1,0},{2,3},{3,2},{4,5},{5,4},{6,7},{7,6},{8,9},{9,8},{10,11... | collective-permute-start | bytes 7864328 | tf_op jit(solution)/shard_map/ppermute | solution.py:25
  353.5 18.3 %collective-permute-start.7 = (f32[4,1280,128]{2,1,0:T(8,128)}, f32[4,1280,128]{2,1,0:T(8,128)}, u32[]{:S(2)}, u32[]{:S(2)}) collective-permute-start(f32[4,1280,128]{2,1,0:T(8,128)} %get-tuple-element.45), channel_id=1, source_target_pairs={{0,1},{1,0},{2,3},{3,2},{4,5},{5,4},{6,7},{7,6},{8,9},{9,8},{10,11... | collective-permute-start | bytes 7864328 | tf_op jit(solution)/shard_map/ppermute | solution.py:25
  353.5 1.6 copy-start.5
  355.0 7.0 %copy-start.8 = (f32[512]{0:T(512)S(1)}, f32[512]{0:T(512)}, u32[]{:S(2)}) copy-start(f32[512]{0:T(512)} %param.11) | copy-start | bytes 6148
  355.0 14.5 %copy-start.3 = (f32[4,1280,128]{2,1,0:T(8,128)S(1)}, f32[4,1280,128]{2,1,0:T(8,128)}, u32[]{:S(2)}) copy-start(f32[4,1280,128]{2,1,0:T(8,128)} %get-tuple-element.44) | copy-start | bytes 7864324
  360.5 66.2 %collective-permute-start.12 = (f32[4,1280,128]{2,1,0:T(8,128)}, f32[4,1280,128]{2,1,0:T(8,128)}, u32[]{:S(2)}, u32[]{:S(2)}) collective-permute-start(f32[4,1280,128]{2,1,0:T(8,128)} %get-tuple-element.73), channel_id=1, source_target_pairs={{0,8},{8,0},{16,24},{24,16},{1,9},{9,1},{17,25},{25,17},{2,10},{10... | collective-permute-start | bytes 7864328 | tf_op jit(solution)/shard_map/ppermute | solution.py:25
  364.9 2.4 collective-permute-start.13
  366.8 2.7 collective-permute-start.11
  369.0 57.0 %collective-permute-start.14 = (f32[1,4,128,128]{3,2,1,0:T(8,128)S(1)}, f32[1,4,128,128]{3,2,1,0:T(8,128)S(1)}, u32[]{:S(2)}, u32[]{:S(2)}) collective-permute-start(f32[1,4,128,128]{3,2,1,0:T(8,128)S(1)} %get-tuple-element.93), channel_id=1, source_target_pairs={{0,8},{8,0},{16,24},{24,16},{1,9},{9,1},{17,25},{25,17},{2,10},{10... | collective-permute-start | bytes 786440 | tf_op jit(solution)/shard_map/ppermute | solution.py:25
  370.2 61.1 %collective-permute-start.15 = (f32[1,4,128,128]{3,2,1,0:T(8,128)S(1)}, f32[1,4,128,128]{3,2,1,0:T(8,128)}, u32[]{:S(2)}, u32[]{:S(2)}) collective-permute-start(f32[1,4,128,128]{3,2,1,0:T(8,128)S(1)} %get-tuple-element.91), channel_id=1, source_target_pairs={{0,8},{8,0},{16,24},{24,16},{1,9},{9,1},{17,25},{25,17},{2,10},{10... | collective-permute-start | bytes 786440 | tf_op jit(solution)/shard_map/ppermute | solution.py:25
  425.9 0.7 copy-start.6
  446.9 7.4 %copy-start.7 = (f32[1,4,128,128]{3,2,1,0:T(8,128)S(1)}, f32[1,4,128,128]{3,2,1,0:T(8,128)}, u32[]{:S(2)}) copy-start(f32[1,4,128,128]{3,2,1,0:T(8,128)} %copy-done.6) | copy-start | bytes 786436
  447.9 2.4 collective-permute-start.20
  452.0 8.7 %collective-permute-start.21 = (f32[1,4,128,128]{3,2,1,0:T(8,128)S(1)}, f32[1,4,128,128]{3,2,1,0:T(8,128)S(1)}, u32[]{:S(2)}, u32[]{:S(2)}) collective-permute-start(f32[1,4,128,128]{3,2,1,0:T(8,128)S(1)} %get-tuple-element.88), channel_id=1, source_target_pairs={{0,8},{8,0},{16,24},{24,16},{1,9},{9,1},{17,25},{25,17},{2,10},{10... | collective-permute-start | bytes 786440 | tf_op jit(solution)/shard_map/ppermute | solution.py:25
  455.0 69.8 %copy-start.2 = (f32[4,1280,128]{2,1,0:T(8,128)S(1)}, f32[4,1280,128]{2,1,0:T(8,128)}, u32[]{:S(2)}) copy-start(f32[4,1280,128]{2,1,0:T(8,128)} %get-tuple-element.48) | copy-start | bytes 7864324
  465.8 168.9 %all-gather.26.cloned.1.call-start = ((), (), s32[]{:S(2)}) async-start(), calls=%async_computation.6 | async-start | bytes 5242880 | tf_op jit(solution)/shard_map/all_gather | solution.py:525
  465.9 58.9 %collective-permute-start.17 = (f32[4,1280,128]{2,1,0:T(8,128)}, f32[4,1280,128]{2,1,0:T(8,128)}, u32[]{:S(2)}, u32[]{:S(2)}) collective-permute-start(f32[4,1280,128]{2,1,0:T(8,128)} %get-tuple-element.75), channel_id=1, source_target_pairs={{0,8},{8,0},{16,24},{24,16},{1,9},{9,1},{17,25},{25,17},{2,10},{10... | collective-permute-start | bytes 7864328 | tf_op jit(solution)/shard_map/ppermute | solution.py:25
  467.5 57.3 %collective-permute-start.16 = (f32[4,1280,128]{2,1,0:T(8,128)}, f32[4,1280,128]{2,1,0:T(8,128)}, u32[]{:S(2)}, u32[]{:S(2)}) collective-permute-start(f32[4,1280,128]{2,1,0:T(8,128)} %get-tuple-element.49), channel_id=1, source_target_pairs={{0,1},{1,0},{2,3},{3,2},{4,5},{5,4},{6,7},{7,6},{8,9},{9,8},{10,11... | collective-permute-start | bytes 7864328 | tf_op jit(solution)/shard_map/ppermute | solution.py:25
  524.7 141.5 %all-gather.28.cloned.1.call-start = ((), (), s32[]{:S(2)}) async-start(), calls=%async_computation.7 | async-start | bytes 2621440 | tf_op jit(solution)/shard_map/all_gather | solution.py:525
  529.4 57.8 %collective-permute-start.18 = (f32[4,1280,128]{2,1,0:T(8,128)}, f32[4,1280,128]{2,1,0:T(8,128)S(1)}, u32[]{:S(2)}, u32[]{:S(2)}) collective-permute-start(f32[4,1280,128]{2,1,0:T(8,128)} %get-tuple-element.71), channel_id=1, source_target_pairs={{0,8},{8,0},{16,24},{24,16},{1,9},{9,1},{17,25},{25,17},{2,10},{10... | collective-permute-start | bytes 7864328 | tf_op jit(solution)/shard_map/ppermute | solution.py:25
  592.5 15.3 %collective-permute-start.19 = (f32[2,2048,128]{2,1,0:T(8,128)}, f32[2,2048,128]{2,1,0:T(8,128)}, u32[]{:S(2)}, u32[]{:S(2)}) collective-permute-start(f32[2,2048,128]{2,1,0:T(8,128)} %west_columns.1.mine_ref), channel_id=1, source_target_pairs={{0,1},{1,0},{2,3},{3,2},{4,5},{5,4},{6,7},{7,6},{8,9},{9,8},{10,11... | collective-permute-start | bytes 6291464 | tf_op jit(solution)/shard_map/ppermute | solution.py:25
  593.7 3.8 collective-permute-start.22
  666.2 19.8 %copy-start.1 = (s32[4,2,40,40]{3,2,1,0:T(8,128)S(1)}, s32[4,2,40,40]{3,2,1,0:T(8,128)}, u32[]{:S(2)}) copy-start(s32[4,2,40,40]{3,2,1,0:T(8,128)} %param.9) | copy-start | bytes 153604
Sparse Core Ops, SparseCore 0:
  11.7 83.4 all-gather.13
  96.7 79.2 all-gather.19
  177.6 79.2 all-gather.15
  258.4 79.2 all-gather.21
  339.1 79.2 all-gather.17
  465.9 44.5 all-gather.23
  524.9 79.3 all-gather.25
  605.9 44.4 all-gather.27
